TPU v7x, 512 devices: a whole 4x8x8 slice. The times are simulated.
512 devices in a mesh: dp: 64 (over x, z, core), tensor: 8 (over y).
Axes of the slice: x: 4, y: 8, z: 8, core: 2. Of those that a mesh axis runs over, the one named last changes fastest.
Arguments:
- finish: int32 [128], P('dp'), may hold values from 0 to 3, as said below
- source: int32 [128], P('dp'), may hold values from 0 to 255, as said below
- ssm_state: float32 [128, 128, 64, 128], P('dp', 'tensor'), may hold values from -6 to 6
- conv_x: bfloat16 [128, 3, 8192], P('dp', None, 'tensor'), may hold values from -6 to 6
- conv_bc: bfloat16 [128, 3, 2, 1024], P('dp', None, None, 'tensor'), may hold values from -6 to 6
- prompt_ssm: bfloat16 [256, 128, 64, 128], P('dp', 'tensor'), may hold values from -6 to 6
- prompt_conv_x: bfloat16 [256, 3, 8192], P('dp', None, 'tensor'), may hold values from -6 to 6
- prompt_conv_bc: bfloat16 [256, 3, 2, 1024], P('dp', None, None, 'tensor'), may hold values from -6 to 6
- x_in: bfloat16 [3, 128, 8192], P(None, 'dp', 'tensor'), may hold values from -6 to 6
- z_in: bfloat16 [3, 128, 8192], P(None, 'dp', 'tensor'), may hold values from -6 to 6
- bc_in: bfloat16 [3, 128, 2, 1024], P(None, 'dp', None, 'tensor'), may hold values from -6 to 6
- dt_in: float32 [3, 128, 128], P(None, 'dp', 'tensor'), may hold values from -6 to 6
- conv_w: float32 [4, 8192], P(None, 'tensor'), may hold values from -3 to 3
- conv_wbc: float32 [4, 2, 1024], P(None, None, 'tensor'), may hold values from -3 to 3
- dt_bias: float32 [128], P('tensor'), may hold values from -4 to -1
- a_log: float32 [128], P('tensor'), may hold values from -1 to 1.5
- skip_d: float32 [128], P('tensor'), may hold values from 0.5 to 1.5
- norm_gain: float32 [8192], P('tensor'), may hold values from 0.5 to 1.5
Outputs:
- outputs: bfloat16 [3, 128, 8192], P(None, 'dp', 'tensor')
- final_state: float32 [128, 128, 64, 128], P('dp', 'tensor')
Inputs may be any that keep to these rules, and one draw needn't show every extreme that they name: `source`: exactly 1 slot of each dp index is refilled (finish below 3); dp indices g that share g // 16 name the same prompt for their refilled slots and others different ones, so each forked prompt refills 16 slots; slots that are not refilled may name any prompt. `finish`: slots that are not refilled have 3.
All inputs are finite; a program needn't handle non-finite values.
Results may differ from a plain program's by a relative error of at most 0.0013.
Values may be sent and summed in bfloat16 or wider, within the bound.
A program may use at most 64 MiB of HBM per device.

v0:
```python
import jax
import jax.numpy as jnp
from jax import lax
from jax.sharding import PartitionSpec as P

H = 128
P_SIZE = 64
FORK = 16
REF_DEV = 1


def body(
    finish,
    source,
    ssm_state,
    conv_x,
    conv_bc,
    prompt_ssm,
    prompt_conv_x,
    prompt_conv_bc,
    x_in,
    z_in,
    bc_in,
    dt_in,
    conv_w,
    conv_wbc,
    dt_bias,
    a_log,
    skip_d,
    norm_gain,
):
    groups = lax.axis_size("dp")
    myself = lax.axis_index("dp")
    slots = finish.shape[0]
    held = prompt_ssm.shape[0]
    steps = x_in.shape[0]
    heads = ssm_state.shape[1]
    width = ssm_state.shape[2]
    states = ssm_state.shape[3]
    group_here = bc_in.shape[3] // states
    span = FORK // REF_DEV
    table_fin, table_src = (
        lax.all_gather(finish, "dp", axis=0, tiled=True),
        lax.all_gather(source, "dp", axis=0, tiled=True),
    )
    table_src = table_src.reshape(groups, slots)
    table_fin = table_fin.reshape(groups, slots)
    group_lead = jnp.sum(jnp.where(table_fin < steps, table_src, 0), axis=1) // REF_DEV
    leaders = group_lead[::span]
    owners = leaders // held
    local_index = leaders % held
    mine = myself // span
    owned = owners == myself
    part_state = jnp.where(
        owned[:, None, None, None],
        jnp.take(prompt_ssm, local_index, axis=0).astype(jnp.float32),
        0.0,
    )
    part_x = jnp.where(
        owned[:, None, None], jnp.take(prompt_conv_x, local_index, axis=0).astype(jnp.float32), 0.0
    )
    part_bc = jnp.where(
        owned[:, None, None, None],
        jnp.take(prompt_conv_bc, local_index, axis=0).astype(jnp.float32),
        0.0,
    )
    summed_state, summed_x, summed_bc = lax.psum((part_state, part_x, part_bc), "dp")
    fork_state = lax.dynamic_index_in_dim(summed_state, mine, 0, keepdims=False)
    fork_x = lax.dynamic_index_in_dim(summed_x, mine, 0, keepdims=False).astype(jnp.bfloat16)
    fork_bc = lax.dynamic_index_in_dim(summed_bc, mine, 0, keepdims=False).astype(jnp.bfloat16)
    state = ssm_state
    win_x_old = conv_x
    win_bc_old = conv_bc
    total_width = H * P_SIZE
    normed_all = []
    for moment in range(steps):
        refill = finish == moment
        state = jnp.where(refill[:, None, None, None], fork_state[None], state)
        win_x_old = jnp.where(refill[:, None, None], fork_x[None], win_x_old)
        win_bc_old = jnp.where(refill[:, None, None, None], fork_bc[None], win_bc_old)
        window_x = jnp.concatenate([win_x_old, x_in[moment][:, None]], axis=1)
        conv_out = jax.nn.silu(jnp.sum(conv_w[None] * window_x.astype(jnp.float32), axis=1))
        win_x_old = window_x[:, 1:]
        window_bc = jnp.concatenate([win_bc_old, bc_in[moment][:, None]], axis=1)
        bc_out = jax.nn.silu(jnp.sum(conv_wbc[None] * window_bc.astype(jnp.float32), axis=1))
        win_bc_old = window_bc[:, 1:]
        step_size = jax.nn.softplus(dt_in[moment] + dt_bias[None])
        decay = jnp.exp(-jnp.exp(a_log)[None] * step_size)
        heads_x = conv_out.reshape(slots, heads, width)
        b_heads = jnp.repeat(
            bc_out[:, 0].reshape(slots, group_here, states), heads // group_here, axis=1
        )
        c_heads = jnp.repeat(
            bc_out[:, 1].reshape(slots, group_here, states), heads // group_here, axis=1
        )
        state = (
            decay[:, :, None, None] * state
            + (step_size[:, :, None] * heads_x)[:, :, :, None] * b_heads[:, :, None, :]
        )
        y_heads = (
            jnp.einsum("shpn,shn->shp", state, c_heads, precision=lax.Precision.HIGHEST)
            + skip_d[None, :, None] * heads_x
        )
        gated = y_heads.reshape(slots, heads * width) * jax.nn.silu(
            z_in[moment].astype(jnp.float32)
        )
        squares = lax.psum(jnp.sum(gated * gated, axis=1), "tensor")
        normed = gated * lax.rsqrt(squares[:, None] / total_width + 1e-05) * norm_gain[None]
        normed_all.append(normed.astype(jnp.bfloat16))
    outputs = jnp.stack(normed_all)
    return (outputs, state)


def solution(mesh):
    return jax.shard_map(
        body,
        mesh=mesh,
        in_specs=(
            P("dp"),
            P("dp"),
            P("dp", "tensor", None, None),
            P("dp", None, "tensor"),
            P("dp", None, None, "tensor"),
            P("dp", "tensor", None, None),
            P("dp", None, "tensor"),
            P("dp", None, None, "tensor"),
            P(None, "dp", "tensor"),
            P(None, "dp", "tensor"),
            P(None, "dp", None, "tensor"),
            P(None, "dp", "tensor"),
            P(None, "tensor"),
            P(None, None, "tensor"),
            P("tensor"),
            P("tensor"),
            P("tensor"),
            P("tensor"),
        ),
        out_specs=(P(None, "dp", "tensor"), P("dp", "tensor", None, None)),
        check_vma=False,
    )
```

profile of v0, /device:TPU:1, one launch (start us, length us, event | category | flops | bytes accessed | tf_op | source)
XLA Modules:
  0.0 316.4 jit_solution(10645484238296254022)
XLA Ops:
  7.2 1.3 dynamic-slice
  9.2 0.9 dynamic-update-slice
  10.1 0.8 dynamic-update-slice.1
  10.9 23.9 %all-reduce.2 = (s32[128]{0:T(128)S(1)}, s32[128]{0:T(128)S(1)}) all-reduce(s32[128]{0:T(128)S(1)} %dynamic-update-slice.1, s32[128]{0:T(128)S(1)} %dynamic-update-slice), channel_id=1, replica_groups=mesh['dp'=64,'tensor'=8] {'dp'}, use_global_device_ids=true, to_apply=%add.1 | all-reduce | flops 256 | bytes 2048
  34.9 0.1 select_n.132
  35.0 0.1 reduce_sum.96
  35.1 0.1 slice.82
  35.3 0.7 gather_fusion
  36.1 1.7 convert_select_fusion
  37.9 0.7 gather_fusion.1
  38.7 0.6 gather_fusion.2
  39.3 245.2 %all-reduce.3 = (bf16[4,3,2,128]{3,2,1,0:T(2,128)(2,1)S(1)}, bf16[4,3,1024]{2,0,1:T(4,128)(2,1)S(1)}) all-reduce(f32[4,3,2,128]{3,2,1,0:T(2,128)S(1)} %convert_select_fusion.2, f32[4,3,1024]{2,0,1:T(4,128)S(1)} %convert_select_fusion.1), channel_id=1, replica_groups=mesh['dp'=64,'tensor'=8] {'dp'}, use_global_device_ids=true, to_apply=%region_4.5 | all-reduce | flops 15360 | bytes 92160 | tf_op jit(solution)/shard_map/psum | solution.py:67
  284.6 0.1 broadcast_select_fusion.2
  284.7 0.1 broadcast_select_fusion.1
  284.8 0.1 broadcast_select_fusion
  284.9 0.1 multiply_reduce_fusion.2
  286.1 1.1 dynamic-slice_bitcast_fusion
  287.2 1.9 fusion
  289.1 2.2 fusion.1
  291.3 1.2 multiply_add_fusion
  292.5 1.7 fusion.28
  294.2 0.2 multiply_reduce_fusion.5
  294.4 14.2 %all-reduce.4 = (f32[2]{0:T(128)S(1)}, f32[2]{0:T(128)S(1)}, f32[2]{0:T(128)S(1)}) all-reduce(f32[2]{0:T(128)S(1)} %get-tuple-element.53, f32[2]{0:T(128)S(1)} %get-tuple-element.51, f32[2]{0:T(128)S(1)} %get-tuple-element.15), channel_id=1, replica_groups=mesh['dp'=64,'tensor'=8] {'tensor'}, use_global_device_ids=true, to_apply=%region_15.16 | all-reduce | flops 6 | bytes 48 | tf_op jit(solution)/shard_map/psum | solution.py:107
  308.9 0.6 pad_maximum_fusion
  (82 shorter events, 1.7 us)
Async XLA Ops:
  7.2 28.1 %copy-start = (bf16[4,16,64,128]{3,2,1,0:T(8,128)(2,1)S(1)}, bf16[4,16,64,128]{3,2,1,0:T(8,128)(2,1)}, u32[]{:S(2)}) copy-start(bf16[4,16,64,128]{3,2,1,0:T(8,128)(2,1)} %param.23) | copy-start | bytes 3145732
  7.2 278.9 %all-reduce.7.cloned.1.call-start = ((), (), s32[]{:S(2)}) async-start(), calls=%async_computation | async-start | bytes 4194304 | tf_op jit(solution)/shard_map/psum | solution.py:67
  36.0 1.8 copy-start.16
  36.0 1.9 copy-start.3
  36.0 2.6 copy-start.8
  37.7 246.9 %copy-start.6 = (bf16[3,2,1024]{2,1,0:T(2,128)(2,1)S(1)}, bf16[3,2,1024]{2,1,0:T(2,128)(2,1)}, u32[]{:S(2)}) copy-start(bf16[3,2,1024]{2,1,0:T(2,128)(2,1)} %param.26) | copy-start | bytes 36868
  37.7 246.9 %copy-start.7 = (bf16[2,3,1024]{2,0,1:T(2,128)(2,1)S(1)}, bf16[2,3,1024]{2,0,1:T(2,128)(2,1)}, u32[]{:S(2)}) copy-start(bf16[2,3,1024]{2,0,1:T(2,128)(2,1)} %param.21) | copy-start | bytes 36868
  37.7 247.2 %copy-start.5 = (f32[4,1024]{1,0:T(4,128)S(1)}, f32[4,1024]{1,0:T(4,128)}, u32[]{:S(2)}) copy-start(f32[4,1024]{1,0:T(4,128)} %param.30) | copy-start | bytes 49156
  37.7 247.4 %copy-start.11 = (bf16[3,2,2,128]{3,2,1,0:T(2,128)(2,1)S(1)}, bf16[3,2,2,128]{3,2,1,0:T(2,128)(2,1)}, u32[]{:S(2)}) copy-start(bf16[3,2,2,128]{3,2,1,0:T(2,128)(2,1)} %param.28) | copy-start | bytes 9220
  37.7 247.4 %copy-start.12 = (bf16[2,3,2,128]{3,2,1,0:T(2,128)(2,1)S(1)}, bf16[2,3,2,128]{3,2,1,0:T(2,128)(2,1)}, u32[]{:S(2)}) copy-start(bf16[2,3,2,128]{3,2,1,0:T(2,128)(2,1)} %param.22) | copy-start | bytes 9220
  37.7 247.7 %copy-start.9 = (f32[4,2,128]{2,1,0:T(2,128)S(1)}, f32[4,2,128]{2,1,0:T(2,128)}, u32[]{:S(2)}) copy-start(f32[4,2,128]{2,1,0:T(2,128)} %param.31) | copy-start | bytes 12292
  37.8 247.8 %copy-start.4 = (bf16[3,2,1024]{2,1,0:T(2,128)(2,1)S(1)}, bf16[3,2,1024]{2,1,0:T(2,128)(2,1)}, u32[]{:S(2)}) copy-start(bf16[3,2,1024]{2,1,0:T(2,128)(2,1)} %param.27) | copy-start | bytes 36868
  37.8 248.1 %copy-start.17 = (f32[16]{0:T(128)S(1)}, f32[16]{0:T(128)}, u32[]{:S(2)}) copy-start(f32[16]{0:T(128)} %param.33) | copy-start | bytes 196
  37.8 248.1 %copy-start.13 = (f32[3,2,16]{2,1,0:T(2,128)S(1)}, f32[3,2,16]{2,1,0:T(2,128)}, u32[]{:S(2)}) copy-start(f32[3,2,16]{2,1,0:T(2,128)} %param.29) | copy-start | bytes 1156
  37.8 248.1 %copy-start.15 = (f32[16]{0:T(128)S(1)}, f32[16]{0:T(128)}, u32[]{:S(2)}) copy-start(f32[16]{0:T(128)} %param.32) | copy-start | bytes 196
  37.8 249.4 %copy-start.1 = (f32[2,16,64,128]{3,2,1,0:T(8,128)S(1)}, f32[2,16,64,128]{3,2,1,0:T(8,128)}, u32[]{:S(2)}) copy-start(f32[2,16,64,128]{3,2,1,0:T(8,128)} %param.20) | copy-start | bytes 3145732
  291.3 2.9 copy-start.14
  291.3 17.5 %copy-start.10 = (f32[1024]{0:T(1024)S(1)}, f32[1024]{0:T(1024)}, u32[]{:S(2)}) copy-start(f32[1024]{0:T(1024)} %param.35) | copy-start | bytes 12292
  292.4 17.1 %copy-start.2 = (f32[2,16,64,128]{3,2,1,0:T(8,128)}, f32[2,16,64,128]{3,2,1,0:T(8,128)S(1)}, u32[]{:S(2)}) copy-start(f32[2,16,64,128]{3,2,1,0:T(8,128)S(1)} %multiply_add_fusion) | copy-start | bytes 3145732
Sparse Core Ops, SparseCore 0:
  38.0 198.0 all-reduce.6
where the time goes:
time: 323 us; the launch traced here: 316 us
  blocking collectives  283 us (88%)
  between operations  15.1 us (5%)
  local copies, waits for them, and re-layouts  7.25 us (2%)
  matrix products  5.8 us (2%)
  other arithmetic  4.85 us (2%)
    psum x1, blocking collectives, body(): lax.psum((part_state, part_x, part_bc), 'dp')  245 us
    unnamed x1, blocking collectives  23.9 us
    psum x1, blocking collectives, body(): squares = lax.psum(jnp.sum(gated * gated, axis=1), 'tensor')  14.2 us
  transfers between devices with their start and end apart: 1, of which 0 were waited for; matrix products, arithmetic and copies ran while one was open for 1% of the time, Pallas kernels for 0%

commit v1 on v0

v1 whole, which is shorter than its diff:
```python
import functools

import jax
import jax.numpy as jnp
from jax import lax
from jax.experimental import pallas as pl
from jax.experimental.pallas import tpu as pltpu
from jax.sharding import PartitionSpec as P

F32 = jnp.float32
BF16 = jnp.bfloat16
MESH = pl.DeviceIdType.MESH
HIGHEST = lax.Precision.HIGHEST

NZ = 8
HELD = 4
HEADS = 16
HALF = 8
WIDTH = 64
STATES = 128
CH = HEADS * WIDTH
LANES = CH + 2 * STATES
STEPS = 3
TAPS = 4
ROWS = 8
TOTAL = 8192
STAGES = ((4, 5), (3, 6), (2, 7), (1, 0))
NEAR = (1, 7, 2, 6, 3, 5, 4)


def silu(v):
    return v * (1.0 / (1.0 + jnp.exp(-v)))


def softplus(v):
    return jnp.maximum(v, 0.0) + jnp.log1p(jnp.exp(-jnp.abs(v)))


def nt(a, b, precision=None):
    return lax.dot_general(
        a, b, (((1,), (1,)), ((), ())), precision=precision, preferred_element_type=F32
    )


def tn(a, b, precision=None):
    return lax.dot_general(
        a, b, (((0,), (0,)), ((), ())), precision=precision, preferred_element_type=F32
    )


def kernel(
    nx,
    ny,
    fin_ref,
    src_ref,
    ssm_hbm,
    cx_hbm,
    cbc_hbm,
    pssm_hbm,
    pcx_hbm,
    pcbc_hbm,
    x_hbm,
    z_hbm,
    bc_hbm,
    dt_hbm,
    cw_hbm,
    cwbc_hbm,
    bias_hbm,
    alog_hbm,
    skip_hbm,
    gain_hbm,
    out_ref,
    fs_hbm,
    ssm,
    cx,
    cbc,
    pcx,
    pcbc,
    xin,
    zin,
    bcin,
    dtin,
    cw,
    cwbc,
    bias,
    alog,
    skip,
    gain,
    plan_out,
    plan_in,
    pbuf,
    pconv,
    cpack,
    csend,
    cxbuf,
    czsend,
    czbuf,
    sbuf,
    xb0,
    xb1,
    xb2,
    xb3,
    zsend,
    zbuf,
    fbuf,
    ysend,
    ybuf,
    seq,
    fork,
    acc,
    wts,
    st,
    ex,
    dec,
    base,
    bco,
    gub,
    ab,
    in_sem,
    own_sem,
    out_sem,
    plan_s,
    plan_r,
    pair_s,
    pair_r,
    cx_s,
    cx_r,
    cz_s,
    cz_r,
    x_s,
    x_r,
    z_s,
    z_r,
    g_s,
    g_r,
    f_s,
    f_r,
    y_s,
    y_r,
):
    me = lax.axis_index("dp")
    c = lax.rem(me, 2)
    z = lax.rem(me // 2, NZ)
    x = me // (2 * NZ)
    y = lax.axis_index("tensor")
    xbs = (xb0, xb1, xb2, xb3)

    def at(xx, zz, cc):
        return {"dp": (xx * NZ + zz) * 2 + cc}

    def xpeer(d):
        return lax.rem(x + d, nx)

    def zpeer(d):
        return lax.rem(z + d, NZ)

    def ypeer(d):
        return lax.rem(y + d, ny)

    sibling = at(x, z, 1 - c)

    def remote(src, dst, ssem, rsem, dev):
        return pltpu.make_async_remote_copy(
            src_ref=src, dst_ref=dst, send_sem=ssem, recv_sem=rsem, device_id=dev, device_id_type=MESH
        )

    mine = pl.ds(pl.multiple_of(c * HALF, HALF), HALF)
    theirs = pl.ds(pl.multiple_of((1 - c) * HALF, HALF), HALF)
    my_slot = pl.ds(pl.multiple_of(c * HELD, HELD), HELD)
    loads = [
        pltpu.make_async_copy(src, dst, in_sem.at[i])
        for i, (src, dst) in enumerate(
            (
                (pcx_hbm, pcx),
                (pcbc_hbm, pcbc),
                (dt_hbm, dtin),
                (bias_hbm, bias),
                (alog_hbm, alog),
                (skip_hbm, skip),
                (cx_hbm, cx),
                (cbc_hbm, cbc),
                (x_hbm, xin),
                (bc_hbm, bcin),
                (cw_hbm, cw),
                (cwbc_hbm, cwbc),
                (z_hbm, zin),
                (gain_hbm, gain),
                (ssm_hbm, ssm),
            )
        )
    ]
    own = pltpu.make_async_copy(pssm_hbm.at[:, mine], pbuf.at[my_slot], own_sem)

    barrier = pltpu.get_barrier_semaphore()
    pl.semaphore_signal(barrier, inc=1, device_id=sibling, device_id_type=MESH)
    for d in range(1, nx):
        pl.semaphore_signal(barrier, inc=1, device_id=at(xpeer(d), z, c), device_id_type=MESH)
    for d in range(1, NZ):
        pl.semaphore_signal(barrier, inc=1, device_id=at(x, zpeer(d), c), device_id_type=MESH)
    for d in range(1, ny):
        pl.semaphore_signal(barrier, inc=1, device_id={"tensor": ypeer(d)}, device_id_type=MESH)
    own.start()
    for cp in loads:
        cp.start()

    fin0, fin1 = fin_ref[0], fin_ref[1]
    prompt = jnp.where(fin0 < STEPS, src_ref[0], src_ref[1])
    plan_out[...] = jnp.full(plan_out.shape, prompt, jnp.int32)
    wts[...] = jnp.zeros_like(wts)
    st[...] = jnp.zeros_like(st)
    acc[...] = jnp.zeros_like(acc)
    base[...] = jnp.zeros_like(base)
    bco[...] = jnp.zeros_like(bco)
    gub[...] = jnp.zeros_like(gub)
    cpack[...] = jnp.zeros_like(cpack)

    pl.semaphore_wait(barrier, 1 + (nx - 1) + (NZ - 1) + (ny - 1))

    plans = {}
    for d in range(1, nx):
        plans[d] = remote(
            plan_out, plan_in.at[d], plan_s.at[d], plan_r.at[d], at(xpeer(d), z, c)
        )
        plans[d].start()
    pair = remote(pssm_hbm.at[:, theirs], pbuf.at[my_slot], pair_s.at[0], pair_r.at[0], sibling)
    pair.start()

    loads[0].wait()
    loads[1].wait()
    for i in range(3):
        tap = pcx[i].astype(F32)
        for q in range(HELD):
            for k in range(8):
                r = 4 * k + i
                cpack[q, r : r + 1, :] = tap[q : q + 1, 128 * k : 128 * (k + 1)]
    for q in range(HELD):
        for i in range(3):
            for b in range(2):
                r = 4 * (2 * i + b) + 3
                cpack[q, r : r + 1, :] = pcbc[q, i, b : b + 1, :].astype(F32)
    pconv[my_slot] = cpack[...].astype(BF16)
    pair_conv = remote(
        pconv.at[my_slot], pconv.at[my_slot], pair_s.at[1], pair_r.at[1], sibling
    )
    pair_conv.start()

    for i in range(2, 6):
        loads[i].wait()
    for t in range(STEPS):
        st[2 * t : 2 * t + 2, :HEADS] = dtin[t]
    st[6:7, :HEADS] = bias[...]
    st[7:8, :HEADS] = alog[...]
    st[8:9, :HEADS] = skip[...]
    small = st[:, :HEADS]
    spread = (
        lax.broadcasted_iota(jnp.int32, (HEADS, CH), 1) // WIDTH
        == lax.broadcasted_iota(jnp.int32, (HEADS, CH), 0)
    ).astype(F32)
    ex[...] = lax.dot_general(
        small, spread, (((1,), (0,)), ((), ())), precision=HIGHEST, preferred_element_type=F32
    )

    for d in range(1, nx):
        plans[d].wait_recv()
    pair.wait_recv()
    pair_conv.wait_recv()
    own.wait()

    def wanted(d):
        return lax.rem(jnp.max(plan_in[nx - d]), 2 * HELD)

    order = (2, 1, 3) if nx == 4 else tuple(range(1, nx))
    want = {d: wanted(d) for d in order}
    want[0] = lax.rem(prompt, 2 * HELD)
    owner_x = prompt // (2 * HELD * NZ)
    owner_z = lax.rem(prompt // (2 * HELD), NZ)

    conv_sends = []
    for i, d in enumerate(order):
        csend[i] = pconv[want[d]]
        cp = remote(csend.at[i], cxbuf.at[x], cx_s.at[d], cx_r.at[d], at(xpeer(d), z, c))
        cp.start()
        conv_sends.append(cp)
    cxbuf[x] = pconv[want[0]]
    x_sends = []
    for g, offsets in enumerate(STAGES):
        sends = []
        for i, d in enumerate(order):
            for n, o in enumerate(offsets):
                sbuf[i, g, n] = pbuf[want[d], zpeer(o)]
            cp = remote(
                sbuf.at[i, g], xbs[g].at[x], x_s.at[g, d], x_r.at[g, d], at(xpeer(d), z, c)
            )
            cp.start()
            sends.append(cp)
        for n, o in enumerate(offsets):
            xbs[g][x, n] = pbuf[want[0], zpeer(o)]
        x_sends.append(sends)

    for i in range(6, 12):
        loads[i].wait()
    for i in range(3):
        seq[i, :, :CH] = cx[i].astype(F32)
        for s in range(2):
            for b in range(2):
                lo = CH + b * STATES
                seq[i, s : s + 1, lo : lo + STATES] = cbc[s, i, b : b + 1, :].astype(F32)
    for t in range(STEPS):
        seq[3 + t, :, :CH] = xin[t].astype(F32)
        for s in range(2):
            for b in range(2):
                lo = CH + b * STATES
                seq[3 + t, s : s + 1, lo : lo + STATES] = bcin[t, s, b : b + 1, :].astype(F32)
    wts[:TAPS, :CH] = cw[...]
    for k in range(TAPS):
        for b in range(2):
            lo = CH + b * STATES
            wts[k : k + 1, lo : lo + STATES] = cwbc[k, b : b + 1, :]

    for cp in conv_sends:
        cp.wait_recv()
    picked = cxbuf[owner_x]
    czsend[...] = picked
    czbuf[z] = picked
    cz_sends = []
    for d in range(1, NZ):
        cp = remote(czsend, czbuf.at[z], cz_s.at[d], cz_r.at[d], at(x, zpeer(d), c))
        cp.start()
        cz_sends.append(cp)

    for t in range(STEPS):
        total = jnp.zeros((2, STATES), F32)
        for k in range(TAPS):
            total += wts[k : k + 1, CH + STATES :] * seq[t + k, :, CH + STATES :]
        acc[2 * t : 2 * t + 2, CH + STATES :] = total
    c_old = silu(acc[:, CH + STATES :])
    loads[14].wait()
    row = lax.broadcasted_iota(jnp.int32, (ROWS, CH), 0)
    y_old = jnp.where(
        lax.rem(row, 2) == 0,
        nt(c_old, ssm[0].reshape(CH, STATES), HIGHEST),
        nt(c_old, ssm[1].reshape(CH, STATES), HIGHEST),
    )
    base[...] = y_old

    z_sends = {}
    for g, offsets in enumerate(STAGES):
        for cp in x_sends[g]:
            cp.wait_recv()
        for n, o in enumerate(offsets):
            head = xbs[g][owner_x, n]
            if o == 0:
                zbuf[z] = head
            else:
                zsend[o] = head
                z_sends[o] = remote(
                    zsend.at[o], zbuf.at[z], z_s.at[o], z_r.at[o], at(x, zpeer(o), c)
                )
                z_sends[o].start()
        if g == 0:
            for cp in cz_sends:
                cp.wait_recv()
            packed = czbuf[owner_z].astype(F32)
            for k in range(8):
                fork[0:3, 128 * k : 128 * (k + 1)] = packed[4 * k : 4 * k + 3]
            for i in range(3):
                for b in range(2):
                    r = 4 * (2 * i + b) + 3
                    lo = CH + b * STATES
                    fork[i : i + 1, lo : lo + STATES] = packed[r : r + 1]
            first = lax.broadcasted_iota(jnp.int32, (2, LANES), 0) == 0
            fin_rows = jnp.where(first, fin0, fin1)
            for t in range(STEPS):
                total = jnp.zeros((2, LANES), F32)
                for k in range(TAPS):
                    w = seq[t + k]
                    for f in range(t + 1):
                        if t + k - f <= 2:
                            r = t + k - f
                            w = jnp.where(fin_rows == f, fork[r : r + 1, :], w)
                    total += wts[k : k + 1, :] * w
                acc[2 * t : 2 * t + 2, :] = total
            acc[...] = silu(acc[...])
        if g == 1:
            step = softplus(ex[0:ROWS] + ex[6:7])
            dec[...] = jnp.exp(-jnp.exp(ex[7:8]) * step)
            ex[0:6] = step[0:6]
            fin_ch = fin_rows[:, :CH]
            a = jnp.ones((2, CH), F32)
            b = jnp.zeros((2, CH), F32)
            gs = []
            for t in range(STEPS):
                two = slice(2 * t, 2 * t + 2)
                now = fin_ch == t
                d_t = dec[two]
                a = jnp.where(now, 0.0, a) * d_t
                b = jnp.where(now, 1.0, b) * d_t
                u = ex[two] * acc[two, :CH]
                gs = [jnp.where(now, 0.0, v) * d_t for v in gs] + [u]
                c_t = acc[two, CH + STATES :]
                total = a * base[two] + ex[8:9] * acc[two, :CH]
                for k in range(t + 1):
                    b_k = acc[2 * k : 2 * k + 2, CH : CH + STATES]
                    total += gs[k] * jnp.sum(b_k * c_t, axis=1, keepdims=True)
                base[two] = total
                bco[two] = b
            for k in range(STEPS):
                gub[2 * k : 2 * k + 2] = gs[k]
        if g == 2:
            pick = (
                lax.broadcasted_iota(jnp.int32, (16, 9 * STATES), 1) // STATES
                == lax.broadcasted_iota(jnp.int32, (16, 9 * STATES), 0)
            ).astype(F32)
            hb = tn(st[:, :HEADS], pick, HIGHEST)

            def col(r):
                return hb[:, r * STATES : (r + 1) * STATES]

            rate = -jnp.exp(col(7))
            for s, fin in enumerate((fin0, fin1)):
                a = jnp.ones((HEADS, STATES), F32)
                b = jnp.zeros((HEADS, STATES), F32)
                fin_v = jnp.full((HEADS, STATES), fin, jnp.int32)
                for t in range(STEPS):
                    d_t = jnp.exp(rate * softplus(col(2 * t + s) + col(6)))
                    a = jnp.where(fin_v == t, 0.0, a) * d_t
                    b = jnp.where(fin_v == t, 1.0, b) * d_t
                ab[0, s] = a
                ab[1, s] = b
            bm = acc[:, CH : CH + STATES]
            odd = lax.rem(lax.broadcasted_iota(jnp.int32, (ROWS, STATES), 0), 2)
            both = jnp.concatenate(
                [jnp.where(odd == 0, bm, 0.0), jnp.where(odd == 1, bm, 0.0)], axis=1
            )
            for h in range(0, HEADS, 4):
                lo = h * WIDTH
                u = tn(gub[:, lo : lo + 4 * WIDTH], both, HIGHEST)
                for j in range(4):
                    for s in range(2):
                        ssm[s, h + j] = (
                            ab[0, s, h + j : h + j + 1, :] * ssm[s, h + j]
                            + u[j * WIDTH : (j + 1) * WIDTH, s * STATES : (s + 1) * STATES]
                        )

    for i in (12, 13):
        loads[i].wait()
    cs = acc[:, CH + STATES :]
    hi = cs.astype(BF16)
    rest = cs - hi.astype(F32)
    mid = rest.astype(BF16)
    low = (rest - mid.astype(F32)).astype(BF16)
    parts = jnp.concatenate(
        [hi.astype(F32), mid.astype(F32), low.astype(F32), jnp.zeros_like(cs)], axis=0
    ).astype(BF16)

    for o in (4, 3, 5, 2, 6, 1, 7):
        z_sends[o].wait_recv()
    here = c * HALF + z
    fbuf[here] = zbuf[owner_z]
    g_sends, f_sends = {}, {}
    for d in (4, 3, 5, 2, 6, 1, 7):
        g_sends[d] = remote(
            fbuf.at[here], fbuf.at[here], g_s.at[d], g_r.at[d], at(x, zpeer(d), c)
        )
        g_sends[d].start()
    f_sends[0] = remote(fbuf.at[here], fbuf.at[here], f_s.at[0], f_r.at[0], sibling)
    f_sends[0].start()
    for d in NEAR:
        g_sends[d].wait_recv()
        landed = c * HALF + zpeer(NZ - d)
        f_sends[d] = remote(fbuf.at[landed], fbuf.at[landed], f_s.at[d], f_r.at[d], sibling)
        f_sends[d].start()
    for d in (0,) + NEAR:
        f_sends[d].wait_recv()

    y_parts = nt(parts, fbuf[...].reshape(CH, STATES))
    y_fork = y_parts[0:8] + y_parts[8:16] + y_parts[16:24]
    gated = base[...] + bco[...] * y_fork
    for t in range(STEPS):
        two = slice(2 * t, 2 * t + 2)
        bco[two] = silu(zin[t].astype(F32))
    gated = gated * bco[...]
    ysend[...] = jnp.broadcast_to(jnp.sum(gated * gated, axis=1, keepdims=True), ysend.shape)
    ybuf[y] = ysend[...]
    y_sends = []
    for d in range(1, ny):
        cp = remote(ysend, ybuf.at[y], y_s.at[d], y_r.at[d], {"tensor": ypeer(d)})
        cp.start()
        y_sends.append(cp)

    stores = []
    for h in range(HEADS):
        f = fbuf[h].astype(F32)
        for s in range(2):
            ssm[s, h] = ssm[s, h] + ab[1, s, h : h + 1, :] * f
        if h % 4 == 3:
            for s in range(2):
                cp = pltpu.make_async_copy(
                    ssm.at[s, h - 3 : h + 1], fs_hbm.at[s, h - 3 : h + 1], out_sem.at[s, h // 4]
                )
                cp.start()
                stores.append(cp)

    for cp in y_sends:
        cp.wait_recv()
    total = ybuf[0]
    for i in range(1, ny):
        total += ybuf[i]
    scale = lax.rsqrt(total[:, 0:1] / TOTAL + 1e-05)
    normed = gated * scale * gain[...]
    for t in range(STEPS):
        out_ref[t] = normed[2 * t : 2 * t + 2].astype(BF16)

    for cp in list(plans.values()) + [pair, pair_conv] + conv_sends + cz_sends + y_sends:
        cp.wait_send()
    for sends in x_sends:
        for cp in sends:
            cp.wait_send()
    for group in (z_sends, g_sends, f_sends):
        for cp in group.values():
            cp.wait_send()
    for cp in stores:
        cp.wait()


def body(nx, ny, *args):
    args = list(args)
    args[3] = jnp.swapaxes(args[3], 0, 1)
    args[6] = jnp.swapaxes(args[6], 0, 1)
    for i in (14, 15, 16, 17):
        args[i] = args[i].reshape(1, -1)
    dma = pltpu.SemaphoreType.DMA
    vmem = pltpu.VMEM
    in_vmem = [args[i] for i in (2, 3, 4, 6, 7, 8, 9, 10, 11, 12, 13, 14, 15, 16, 17)]
    head = (WIDTH, STATES)
    scratch = [vmem(a.shape, a.dtype) for a in in_vmem]
    scratch += [
        vmem((8, 128), jnp.int32),
        vmem((nx, 8, 128), jnp.int32),
        vmem((2 * HELD, HALF) + head, BF16),
        vmem((2 * HELD, 32, 128), BF16),
        vmem((HELD, 32, 128), F32),
        vmem((nx, 32, 128), BF16),
        vmem((nx, 32, 128), BF16),
        vmem((32, 128), BF16),
        vmem((NZ, 32, 128), BF16),
        vmem((nx, 4, 2) + head, BF16),
    ]
    scratch += [vmem((nx, 2) + head, BF16) for _ in range(4)]
    scratch += [
        vmem((NZ,) + head, BF16),
        vmem((NZ,) + head, BF16),
        vmem((HEADS,) + head, BF16),
        vmem((8, 128), F32),
        vmem((ny, 8, 128), F32),
        vmem((6, 2, LANES), F32),
        vmem((8, LANES), F32),
        vmem((ROWS, LANES), F32),
        vmem((8, LANES), F32),
        vmem((16, 128), F32),
        vmem((16, CH), F32),
        vmem((ROWS, CH), F32),
        vmem((ROWS, CH), F32),
        vmem((ROWS, CH), F32),
        vmem((ROWS, CH), F32),
        vmem((2, 2, HEADS, STATES), F32),
        dma((len(in_vmem),)),
        dma,
        dma((2, 4)),
        dma((nx,)),
        dma((nx,)),
        dma((2,)),
        dma((2,)),
        dma((nx,)),
        dma((nx,)),
        dma((NZ,)),
        dma((NZ,)),
        dma((4, nx)),
        dma((4, nx)),
        dma((NZ,)),
        dma((NZ,)),
        dma((NZ,)),
        dma((NZ,)),
        dma((NZ,)),
        dma((NZ,)),
        dma((ny,)),
        dma((ny,)),
    ]
    anywhere = pl.BlockSpec(memory_space=pl.ANY)
    scalars = pl.BlockSpec(memory_space=pltpu.SMEM)
    slots = args[0].shape[0]
    return pl.pallas_call(
        functools.partial(kernel, nx, ny),
        out_shape=(
            jax.ShapeDtypeStruct((STEPS, slots, CH), BF16),
            jax.ShapeDtypeStruct(args[2].shape, F32),
        ),
        in_specs=[scalars, scalars] + [anywhere] * 16,
        out_specs=(pl.BlockSpec(memory_space=pltpu.VMEM), anywhere),
        scratch_shapes=scratch,
        compiler_params=pltpu.CompilerParams(
            collective_id=0, has_side_effects=True, vmem_limit_bytes=60 * 1024 * 1024
        ),
    )(*args)


def solution(mesh):
    nx = mesh.shape["dp"] // (2 * NZ)
    ny = mesh.shape["tensor"]
    return jax.shard_map(
        functools.partial(body, nx, ny),
        mesh=mesh,
        in_specs=(
            P("dp"),
            P("dp"),
            P("dp", "tensor", None, None),
            P("dp", None, "tensor"),
            P("dp", None, None, "tensor"),
            P("dp", "tensor", None, None),
            P("dp", None, "tensor"),
            P("dp", None, None, "tensor"),
            P(None, "dp", "tensor"),
            P(None, "dp", "tensor"),
            P(None, "dp", None, "tensor"),
            P(None, "dp", "tensor"),
            P(None, "tensor"),
            P(None, None, "tensor"),
            P("tensor"),
            P("tensor"),
            P("tensor"),
            P("tensor"),
        ),
        out_specs=(P(None, "dp", "tensor"), P("dp", "tensor", None, None)),
        check_vma=False,
    )
```

time: 323 us -> 49.1 us (0.15); the launches traced: 316 us -> 48.9 us
  blocking collectives: 283 us -> 0 us
  Pallas kernels: 0 us -> 44.6 us
  between operations: 15.1 us -> 0.65 us
  matrix products: 5.8 us -> 0 us
  other arithmetic: 4.85 us -> 0 us
  local copies, waits for them, and re-layouts: 7.25 us -> 3.62 us
    psum x2 -> x0, blocking collectives: 259 us -> none  [the longest x1 245 us: body(): lax.psum((part_state, part_x, part_bc), 'dp')]
    pallas_call x0 -> x1, Pallas kernels: none -> 44.6 us  [body(): pl.pallas_call(functools.partial(kernel, nx, ny), out_shape=(jax.ShapeDty...]
    unnamed x1 -> x0, blocking collectives: 23.9 us -> none
    dot_general x3 -> x0, matrix products: 5.8 us -> none  [body(): jnp.einsum('shpn,shn->shp', state, c_heads, precision=lax.Precision.HIGHEST)]
  transfers between devices with their start and end apart: 1 -> 0, of which waited for: 0 -> 0; matrix products, arithmetic and copies ran while one was open for 1% -> 0% of each run, Pallas kernels for 0% -> 0%
where the time goes in v1:
time: 49.1 us; the launch traced here: 48.9 us
  Pallas kernels  44.6 us (91%)
  local copies, waits for them, and re-layouts  3.62 us (7%)
  between operations  0.65 us (1%)
    pallas_call x1, Pallas kernels, body(): pl.pallas_call(functools.partial(kernel, nx, ny), out_shape=(jax.ShapeDty...  44.6 us
    unnamed x2, local copies, waits for them, and re-layouts  3.62 us

profile of v1, /device:TPU:1, one launch (start us, length us, event | category | flops | bytes accessed | tf_op | source)
XLA Modules:
  0.0 48.9 jit_solution(433775848280957849)
XLA Ops:
  0.6 44.6 %shard_map.185 = (bf16[3,2,1024]{2,1,0:T(2,128)(2,1)}, f32[2,16,64,128]{3,2,1,0:T(8,128)}) custom-call(s32[2]{0:T(128)} %fin_ref.1, s32[2]{0:T(128)} %src_ref.1, f32[2,16,64,128]{3,2,1,0:T(8,128)} %ssm_hbm.1, bf16[3,2,1024]{2,1,0:T(2,128)(2,1)} %bitcast.7, bf16[2,3,2,128]{3,2,1,0:T(2,128)(2,1)} %cbc_hbm.1, bf16[4,16,64,128]{3,2,1,0:T(8,128)(2,1)} %pssm_hbm.1, ...), custom_call_target="tpu_custom_call" | custom-call | tf_op jit(solution)/shard_map/pallas_call | solution.py:592
  45.3 1.3 %copy.22 = bf16[3,2,1024]{2,1,0:T(2,128)(2,1)} copy(bf16[3,2,1024]{2,1,0:T(2,128)(2,1)} %get-tuple-element.4) | data formatting | bytes 24576
  46.6 2.3 %copy.23 = f32[2,16,64,128]{3,2,1,0:T(8,128)} copy(f32[2,16,64,128]{3,2,1,0:T(8,128)} %get-tuple-element.5) | data formatting | bytes 2097152

commit v2 on v0

v2 whole, which is shorter than its diff:
```python
import functools

import jax
import jax.numpy as jnp
from jax import lax
from jax.experimental import pallas as pl
from jax.experimental.pallas import tpu as pltpu
from jax.sharding import PartitionSpec as P

F32 = jnp.float32
BF16 = jnp.bfloat16
MESH = pl.DeviceIdType.MESH

NZ = 8
HELD = 4
HEADS = 16
HALF = 8
WIDTH = 64
STATES = 128
CH = HEADS * WIDTH
LANES = CH + 2 * STATES
STEPS = 3
TAPS = 4
ROWS = 8
TOTAL = 8192
STAGES = ((4, 3, 5), (2, 6, 7), (1, 0))
NEAR = (1, 7, 2, 6, 3, 5, 4)


def silu(v):
    return v * (1.0 / (1.0 + jnp.exp(-v)))


def softplus(v):
    return jnp.maximum(v, 0.0) + jnp.log1p(jnp.exp(-jnp.abs(v)))


def dot(a, b, da, db):
    return lax.dot_general(a, b, (((da,), (db,)), ((), ())), preferred_element_type=F32)


def split(v, n):
    parts = []
    for _ in range(n):
        hi = v.astype(BF16).astype(F32)
        parts.append(hi)
        v = v - hi
    return parts


def stack(parts, axis):
    return jnp.concatenate(parts, axis=axis).astype(BF16)


def sec_pack(R):
    for i in range(3):
        tap = R.pcx[i].astype(F32)
        for q in range(HELD):
            for k in range(8):
                r = 4 * k + i
                R.cpack[q, r : r + 1, :] = tap[q : q + 1, 128 * k : 128 * (k + 1)]
    for q in range(HELD):
        for i in range(3):
            for b in range(2):
                r = 4 * (2 * i + b) + 3
                R.cpack[q, r : r + 1, :] = R.pcbc[q, i, b : b + 1, :].astype(F32)


def sec_dt(R):
    for t in range(STEPS):
        R.st[2 * t : 2 * t + 2, :HEADS] = R.dtin[t]
    R.st[6:7, :HEADS] = R.bias[...]
    R.st[7:8, :HEADS] = R.alog[...]
    R.st[8:9, :HEADS] = R.skip[...]
    parts = split(R.st[:, :HEADS], 3)
    spread = (
        lax.broadcasted_iota(jnp.int32, (HEADS, CH), 1) // WIDTH
        == lax.broadcasted_iota(jnp.int32, (HEADS, CH), 0)
    ).astype(F32)
    full = dot(stack(parts, 1), stack([spread] * 3, 0), 1, 0)
    step = softplus(full[0:ROWS] + full[6:7])
    R.ex[0:ROWS] = step
    R.ex[8:9] = full[8:9]
    R.dec[...] = jnp.exp(-jnp.exp(full[7:8]) * step)


def sec_ab(R):
    pick = (
        lax.broadcasted_iota(jnp.int32, (16, 8 * STATES), 1) // STATES
        == lax.broadcasted_iota(jnp.int32, (16, 8 * STATES), 0)
    ).astype(F32)
    parts = split(R.st[:, :HEADS], 3)
    hb = dot(stack(parts, 0), stack([pick] * 3, 0), 0, 0)

    def col(r):
        return hb[:, r * STATES : (r + 1) * STATES]

    rate = -jnp.exp(col(7))
    for s in range(2):
        a = jnp.ones((HEADS, STATES), F32)
        b = jnp.zeros((HEADS, STATES), F32)
        fin = jnp.full((HEADS, STATES), R.fin[s], jnp.int32)
        for t in range(STEPS):
            d_t = jnp.exp(rate * softplus(col(2 * t + s) + col(6)))
            a = jnp.where(fin == t, 0.0, a) * d_t
            b = jnp.where(fin == t, 1.0, b) * d_t
        R.ab[0, s] = a
        R.ab[1, s] = b


def sec_seq(R):
    for i in range(3):
        R.seq[i, :, :CH] = R.cx[i].astype(F32)
        for s in range(2):
            for b in range(2):
                lo = CH + b * STATES
                R.seq[i, s : s + 1, lo : lo + STATES] = R.cbc[s, i, b : b + 1, :].astype(F32)
    for t in range(STEPS):
        R.seq[3 + t, :, :CH] = R.xin[t].astype(F32)
        for s in range(2):
            for b in range(2):
                lo = CH + b * STATES
                R.seq[3 + t, s : s + 1, lo : lo + STATES] = R.bcin[t, s, b : b + 1, :].astype(F32)
    R.wts[:TAPS, :CH] = R.cw[...]
    for k in range(TAPS):
        for b in range(2):
            lo = CH + b * STATES
            R.wts[k : k + 1, lo : lo + STATES] = R.cwbc[k, b : b + 1, :]


def sec_old(R):
    for t in range(STEPS):
        total = jnp.zeros((2, STATES), F32)
        for k in range(TAPS):
            total += R.wts[k : k + 1, CH + STATES :] * R.seq[t + k, :, CH + STATES :]
        R.acc[2 * t : 2 * t + 2, CH + STATES :] = total
    c_hi, c_lo = split(silu(R.acc[:, CH + STATES :]), 2)
    c_parts = stack([c_hi, c_lo], 0)
    ys = []
    for s in range(2):
        state = R.ssm[s].reshape(CH, STATES)
        hi = state.astype(BF16)
        lo = (state - hi.astype(F32)).astype(BF16)
        both = dot(c_parts, hi, 1, 1)
        ys.append(both[0:ROWS] + both[ROWS:] + dot(c_parts, lo, 1, 1)[0:ROWS])
    row = lax.broadcasted_iota(jnp.int32, (ROWS, CH), 0)
    R.base[...] = jnp.where(lax.rem(row, 2) == 0, ys[0], ys[1])


def sec_unpack(R, packed):
    for k in range(8):
        R.fork[0:3, 128 * k : 128 * (k + 1)] = packed[4 * k : 4 * k + 3]
    for i in range(3):
        for b in range(2):
            r = 4 * (2 * i + b) + 3
            lo = CH + b * STATES
            R.fork[i : i + 1, lo : lo + STATES] = packed[r : r + 1]


def fin_rows(R, lanes):
    first = lax.broadcasted_iota(jnp.int32, (2, lanes), 0) == 0
    return jnp.where(first, R.fin[0], R.fin[1])


def sec_conv(R):
    fin = fin_rows(R, LANES)
    for t in range(STEPS):
        total = jnp.zeros((2, LANES), F32)
        for k in range(TAPS):
            w = R.seq[t + k]
            for f in range(t + 1):
                if t + k - f <= 2:
                    r = t + k - f
                    w = jnp.where(fin == f, R.fork[r : r + 1, :], w)
            total += R.wts[k : k + 1, :] * w
        R.acc[2 * t : 2 * t + 2, :] = total
    R.acc[...] = silu(R.acc[...])


def sec_mix(R):
    fin = fin_rows(R, CH)
    a = jnp.ones((2, CH), F32)
    b = jnp.zeros((2, CH), F32)
    gs = []
    for t in range(STEPS):
        two = slice(2 * t, 2 * t + 2)
        now = fin == t
        d_t = R.dec[two]
        a = jnp.where(now, 0.0, a) * d_t
        b = jnp.where(now, 1.0, b) * d_t
        x_t = R.acc[two, :CH]
        u = R.ex[two] * x_t
        gs = [jnp.where(now, 0.0, v) * d_t for v in gs] + [u]
        c_t = R.acc[two, CH + STATES :]
        total = a * R.base[two] + R.ex[8:9] * x_t
        for k in range(t + 1):
            b_k = R.acc[2 * k : 2 * k + 2, CH : CH + STATES]
            total += gs[k] * jnp.sum(b_k * c_t, axis=1, keepdims=True)
        R.base[two] = total
        R.bco[two] = b
    for k in range(STEPS):
        R.gub[2 * k : 2 * k + 2] = gs[k]
    for t in range(STEPS):
        R.gate[2 * t : 2 * t + 2] = silu(R.zin[t].astype(F32))
    R.cparts[...] = stack(split(R.acc[:, CH + STATES :], 3) + [jnp.zeros((ROWS, STATES), F32)], 0)


def sec_last(R):
    bm = R.acc[:, CH : CH + STATES]
    odd = lax.rem(lax.broadcasted_iota(jnp.int32, (ROWS, STATES), 0), 2)
    both = jnp.concatenate([jnp.where(odd == 0, bm, 0.0), jnp.where(odd == 1, bm, 0.0)], axis=1)
    b_hi, b_lo = split(both, 2)
    g_hi, g_lo = split(R.gub[...], 2)
    rhs = stack([b_hi, b_hi, b_lo, b_lo], 0)
    lhs = stack([g_hi, g_lo, g_hi, g_lo], 0)
    u = dot(lhs, rhs, 0, 0)
    for h in range(HEADS):
        for s in range(2):
            R.ssm[s, h] = (
                R.ab[0, s, h : h + 1, :] * R.ssm[s, h]
                + u[h * WIDTH : (h + 1) * WIDTH, s * STATES : (s + 1) * STATES]
            )


def sec_gate(R):
    y = dot(R.cparts[...], R.fbuf[...].reshape(CH, STATES), 1, 1)
    y = y[0:8] + y[8:16] + y[16:24]
    gated = (R.base[...] + R.bco[...] * y) * R.gate[...]
    R.base[...] = gated
    return jnp.sum(gated * gated, axis=1, keepdims=True)


def sec_state(R, h):
    f = R.fbuf[h].astype(F32)
    for s in range(2):
        R.ssm[s, h] = R.ssm[s, h] + R.ab[1, s, h : h + 1, :] * f


NAMES = (
    "fin_hbm",
    "src_hbm",
    "ssm_hbm",
    "cx_hbm",
    "cbc_hbm",
    "pssm_hbm",
    "pcx_hbm",
    "pcbc_hbm",
    "x_hbm",
    "z_hbm",
    "bc_hbm",
    "dt_hbm",
    "cw_hbm",
    "cwbc_hbm",
    "bias_hbm",
    "alog_hbm",
    "skip_hbm",
    "gain_hbm",
    "out",
    "fs_hbm",
    "ssm",
    "cx",
    "cbc",
    "pcx",
    "pcbc",
    "xin",
    "zin",
    "bcin",
    "dtin",
    "cw",
    "cwbc",
    "bias",
    "alog",
    "skip",
    "gain",
    "fin",
    "src",
    "plan_out",
    "plan_in",
    "pbuf",
    "pconv",
    "cpack",
    "csend",
    "cxbuf",
    "czsend",
    "czbuf",
    "sbuf",
    *(f"xb{g}" for g in range(len(STAGES))),
    "zsend",
    "zbuf",
    "fbuf",
    "ysend",
    "ybuf",
    "seq",
    "fork",
    "acc",
    "wts",
    "st",
    "ex",
    "dec",
    "base",
    "bco",
    "gub",
    "gate",
    "ab",
    "cparts",
    "in_sem",
    "sc_sem",
    "own_sem",
    "out_sem",
    "plan_s",
    "plan_r",
    "pair_s",
    "pair_r",
    "cx_s",
    "cx_r",
    "cz_s",
    "cz_r",
    "x_s",
    "x_r",
    "z_s",
    "z_r",
    "g_s",
    "g_r",
    "f_s",
    "f_r",
    "y_s",
    "y_r",
)


class Refs:
    pass


def kernel(nx, ny, *refs):
    R = Refs()
    for name, ref in zip(NAMES, refs, strict=True):
        setattr(R, name, ref)
    me = lax.axis_index("dp")
    c = lax.rem(me, 2)
    z = lax.rem(me // 2, NZ)
    x = me // (2 * NZ)
    y = lax.axis_index("tensor")
    xbs = [getattr(R, f"xb{g}") for g in range(len(STAGES))]

    def at(xx, zz, cc):
        return {"dp": (xx * NZ + zz) * 2 + cc}

    def xpeer(d):
        return lax.rem(x + d, nx)

    def zpeer(d):
        return lax.rem(z + d, NZ)

    def ypeer(d):
        return lax.rem(y + d, ny)

    sibling = at(x, z, 1 - c)

    def remote(src, dst, ssem, rsem, dev):
        return pltpu.make_async_remote_copy(
            src_ref=src, dst_ref=dst, send_sem=ssem, recv_sem=rsem, device_id=dev, device_id_type=MESH
        )

    barrier = pltpu.get_barrier_semaphore()
    for d in range(1, ny):
        pl.semaphore_signal(barrier, inc=1, device_id={"tensor": ypeer(d)}, device_id_type=MESH)
    for d in range(1, NZ):
        pl.semaphore_signal(barrier, inc=1, device_id=at(x, zpeer(d), c), device_id_type=MESH)
    for d in range(1, nx):
        pl.semaphore_signal(barrier, inc=1, device_id=at(xpeer(d), z, c), device_id_type=MESH)
    pl.semaphore_signal(barrier, inc=1, device_id=sibling, device_id_type=MESH)

    mine = pl.ds(pl.multiple_of(c * HALF, HALF), HALF)
    theirs = pl.ds(pl.multiple_of((1 - c) * HALF, HALF), HALF)
    my_slot = pl.ds(pl.multiple_of(c * HELD, HELD), HELD)
    scalars = [
        pltpu.make_async_copy(R.fin_hbm, R.fin, R.sc_sem.at[0]),
        pltpu.make_async_copy(R.src_hbm, R.src, R.sc_sem.at[1]),
    ]
    loads = [
        pltpu.make_async_copy(src, dst, R.in_sem.at[i])
        for i, (src, dst) in enumerate(
            (
                (R.pcx_hbm, R.pcx),
                (R.pcbc_hbm, R.pcbc),
                (R.dt_hbm, R.dtin),
                (R.bias_hbm, R.bias),
                (R.alog_hbm, R.alog),
                (R.skip_hbm, R.skip),
                (R.cx_hbm, R.cx),
                (R.cbc_hbm, R.cbc),
                (R.x_hbm, R.xin),
                (R.bc_hbm, R.bcin),
                (R.cw_hbm, R.cw),
                (R.cwbc_hbm, R.cwbc),
                (R.z_hbm, R.zin),
                (R.gain_hbm, R.gain),
                (R.ssm_hbm, R.ssm),
            )
        )
    ]
    own = pltpu.make_async_copy(R.pssm_hbm.at[:, mine], R.pbuf.at[my_slot], R.own_sem)
    for cp in scalars + loads[:2] + [own] + loads[2:]:
        cp.start()
    for ref in (R.wts, R.st, R.acc, R.base, R.bco, R.gub, R.gate):
        ref[...] = jnp.zeros_like(ref)
    for cp in scalars:
        cp.wait()
    prompt = jnp.where(R.fin[0] < STEPS, R.src[0], R.src[1])
    R.plan_out[...] = jnp.full(R.plan_out.shape, prompt, jnp.int32)

    pl.semaphore_wait(barrier, 1 + (nx - 1) + (NZ - 1) + (ny - 1))

    order = (2, 1, 3) if nx == 4 else tuple(range(1, nx))
    plans = {}
    for d in order:
        plans[d] = remote(
            R.plan_out, R.plan_in.at[d], R.plan_s.at[d], R.plan_r.at[d], at(xpeer(d), z, c)
        )
        plans[d].start()
    pair = remote(R.pssm_hbm.at[:, theirs], R.pbuf.at[my_slot], R.pair_s.at[0], R.pair_r.at[0], sibling)
    pair.start()
    loads[0].wait()
    loads[1].wait()
    sec_pack(R)
    R.pconv[my_slot] = R.cpack[...].astype(BF16)
    pair_conv = remote(
        R.pconv.at[my_slot], R.pconv.at[my_slot], R.pair_s.at[1], R.pair_r.at[1], sibling
    )
    pair_conv.start()

    for i in range(2, 6):
        loads[i].wait()
    sec_dt(R)
    sec_ab(R)

    pair.wait_recv()
    pair_conv.wait_recv()
    own.wait()
    for d in order:
        plans[d].wait_recv()

    def wanted(d):
        return lax.rem(jnp.max(R.plan_in[nx - d]), 2 * HELD)

    want = {d: wanted(d) for d in order}
    want[0] = lax.rem(prompt, 2 * HELD)
    owner_x = prompt // (2 * HELD * NZ)
    owner_z = lax.rem(prompt // (2 * HELD), NZ)

    conv_sends = []
    for i, d in enumerate(order):
        R.csend[i] = R.pconv[want[d]]
        cp = remote(R.csend.at[i], R.cxbuf.at[x], R.cx_s.at[d], R.cx_r.at[d], at(xpeer(d), z, c))
        cp.start()
        conv_sends.append(cp)
    starts = [sum(len(o) for o in STAGES[:g]) for g in range(len(STAGES))]
    x_sends = []
    for g, offsets in enumerate(STAGES):
        sends = []
        for i, d in enumerate(order):
            for n, o in enumerate(offsets):
                R.sbuf[i, starts[g] + n] = R.pbuf[want[d], zpeer(o)]
            part = R.sbuf.at[i, starts[g] : starts[g] + len(offsets)]
            cp = remote(
                part, xbs[g].at[x], R.x_s.at[g, d], R.x_r.at[g, d], at(xpeer(d), z, c)
            )
            cp.start()
            sends.append(cp)
        x_sends.append(sends)
    R.cxbuf[x] = R.pconv[want[0]]
    for g, offsets in enumerate(STAGES):
        for n, o in enumerate(offsets):
            xbs[g][x, n] = R.pbuf[want[0], zpeer(o)]

    for i in range(6, 12):
        loads[i].wait()
    sec_seq(R)

    for cp in conv_sends:
        cp.wait_recv()
    picked = R.cxbuf[owner_x]
    R.czsend[...] = picked
    R.czbuf[z] = picked
    cz_sends = []
    for d in (4, 3, 5, 2, 6, 1, 7):
        cp = remote(R.czsend, R.czbuf.at[z], R.cz_s.at[d], R.cz_r.at[d], at(x, zpeer(d), c))
        cp.start()
        cz_sends.append(cp)
    loads[14].wait()
    sec_old(R)

    z_sends = {}
    for g, offsets in enumerate(STAGES):
        for cp in x_sends[g]:
            cp.wait_recv()
        for n, o in enumerate(offsets):
            head = xbs[g][owner_x, n]
            if o == 0:
                R.zbuf[z] = head
            else:
                R.zsend[o] = head
                z_sends[o] = remote(
                    R.zsend.at[o], R.zbuf.at[z], R.z_s.at[o], R.z_r.at[o], at(x, zpeer(o), c)
                )
                z_sends[o].start()

    for cp in cz_sends:
        cp.wait_recv()
    sec_unpack(R, R.czbuf[owner_z].astype(F32))
    sec_conv(R)

    for o in (4, 3, 5, 2, 6, 1, 7):
        z_sends[o].wait_recv()
    here = c * HALF + z
    R.fbuf[here] = R.zbuf[owner_z]
    g_sends, f_sends = {}, {}
    for d in (4, 3, 5, 2, 6, 1, 7):
        g_sends[d] = remote(
            R.fbuf.at[here], R.fbuf.at[here], R.g_s.at[d], R.g_r.at[d], at(x, zpeer(d), c)
        )
        g_sends[d].start()
    f_sends[0] = remote(R.fbuf.at[here], R.fbuf.at[here], R.f_s.at[0], R.f_r.at[0], sibling)
    f_sends[0].start()
    for i in (12, 13):
        loads[i].wait()
    sec_mix(R)
    sec_last(R)
    for d in NEAR:
        g_sends[d].wait_recv()
        landed = c * HALF + zpeer(NZ - d)
        f_sends[d] = remote(R.fbuf.at[landed], R.fbuf.at[landed], R.f_s.at[d], R.f_r.at[d], sibling)
        f_sends[d].start()
    for d in (0,) + NEAR:
        f_sends[d].wait_recv()

    squares = sec_gate(R)
    R.ysend[...] = jnp.broadcast_to(squares, R.ysend.shape)
    R.ybuf[y] = R.ysend[...]
    y_sends = []
    for d in (4, 3, 5, 2, 6, 1, 7) if ny == 8 else range(1, ny):
        cp = remote(R.ysend, R.ybuf.at[y], R.y_s.at[d], R.y_r.at[d], {"tensor": ypeer(d)})
        cp.start()
        y_sends.append(cp)

    stores = []
    for h in range(HEADS):
        sec_state(R, h)
        if h % 4 == 3:
            for s in range(2):
                some = slice(h - 3, h + 1)
                cp = pltpu.make_async_copy(
                    R.ssm.at[s, some], R.fs_hbm.at[s, some], R.out_sem.at[s, h // 4]
                )
                cp.start()
                stores.append(cp)
    for cp in list(plans.values()) + [pair, pair_conv] + conv_sends + cz_sends:
        cp.wait_send()
    for sends in x_sends:
        for cp in sends:
            cp.wait_send()
    for group in (z_sends, g_sends, f_sends):
        for cp in group.values():
            cp.wait_send()
    for cp in stores:
        cp.wait()

    for cp in y_sends:
        cp.wait_recv()
    total = R.ybuf[0]
    for i in range(1, ny):
        total += R.ybuf[i]
    scale = lax.rsqrt(total[:, 0:1] / TOTAL + 1e-05)
    normed = R.base[...] * scale * R.gain[...]
    for t in range(STEPS):
        R.out[t] = normed[2 * t : 2 * t + 2].astype(BF16)
    for cp in y_sends:
        cp.wait_send()


def put(out_ref, fs_ref, out_hbm, fs_hbm, sem):
    copies = [
        pltpu.make_async_copy(fs_ref.at[s, h : h + 8], fs_hbm.at[s, h : h + 8], sem.at[2 * s + h // 8])
        for s in range(2)
        for h in (0, 8)
    ]
    copies.append(pltpu.make_async_copy(out_ref, out_hbm, sem.at[4]))
    for cp in copies:
        cp.start()
    for cp in copies:
        cp.wait()


def body(nx, ny, *args):
    args = list(args)
    args[3] = jnp.swapaxes(args[3], 0, 1)
    args[6] = jnp.swapaxes(args[6], 0, 1)
    for i in (14, 15, 16, 17):
        args[i] = args[i].reshape(1, -1)
    dma = pltpu.SemaphoreType.DMA
    vmem = pltpu.VMEM
    in_vmem = [args[i] for i in (2, 3, 4, 6, 7, 8, 9, 10, 11, 12, 13, 14, 15, 16, 17)]
    head = (WIDTH, STATES)
    scratch = [vmem(a.shape, a.dtype) for a in in_vmem]
    scratch += [pltpu.SMEM(a.shape, a.dtype) for a in args[:2]]
    scratch += [
        vmem((8, 128), jnp.int32),
        vmem((nx, 8, 128), jnp.int32),
        vmem((2 * HELD, HALF) + head, BF16),
        vmem((2 * HELD, 32, 128), BF16),
        vmem((HELD, 32, 128), F32),
        vmem((nx, 32, 128), BF16),
        vmem((nx, 32, 128), BF16),
        vmem((32, 128), BF16),
        vmem((NZ, 32, 128), BF16),
        vmem((nx, NZ) + head, BF16),
    ]
    scratch += [vmem((nx, len(o)) + head, BF16) for o in STAGES]
    scratch += [
        vmem((NZ,) + head, BF16),
        vmem((NZ,) + head, BF16),
        vmem((HEADS,) + head, BF16),
        vmem((8, 128), F32),
        vmem((ny, 8, 128), F32),
        vmem((6, 2, LANES), F32),
        vmem((8, LANES), F32),
        vmem((ROWS, LANES), F32),
        vmem((8, LANES), F32),
        vmem((16, 128), F32),
        vmem((16, CH), F32),
        vmem((ROWS, CH), F32),
        vmem((ROWS, CH), F32),
        vmem((ROWS, CH), F32),
        vmem((ROWS, CH), F32),
        vmem((ROWS, CH), F32),
        vmem((2, 2, HEADS, STATES), F32),
        vmem((4 * ROWS, STATES), BF16),
        dma((len(in_vmem),)),
        dma((2,)),
        dma,
        dma((2, 4)),
        dma((nx,)),
        dma((nx,)),
        dma((2,)),
        dma((2,)),
        dma((nx,)),
        dma((nx,)),
        dma((NZ,)),
        dma((NZ,)),
        dma((len(STAGES), nx)),
        dma((len(STAGES), nx)),
        dma((NZ,)),
        dma((NZ,)),
        dma((NZ,)),
        dma((NZ,)),
        dma((NZ,)),
        dma((NZ,)),
        dma((ny,)),
        dma((ny,)),
    ]
    args = [pltpu.with_memory_space_constraint(a, pltpu.HBM) for a in args]
    anywhere = pl.BlockSpec(memory_space=pl.ANY)
    slots = args[0].shape[0]
    out, fs = pl.pallas_call(
        functools.partial(kernel, nx, ny),
        out_shape=(
            pltpu.VMEM((STEPS, slots, CH), BF16),
            pltpu.VMEM(args[2].shape, F32),
        ),
        in_specs=[anywhere] * 18,
        out_specs=(pl.BlockSpec(memory_space=pltpu.VMEM), anywhere),
        scratch_shapes=scratch,
        compiler_params=pltpu.CompilerParams(
            collective_id=0, has_side_effects=True, vmem_limit_bytes=32 * 1024 * 1024
        ),
    )(*args)
    return pl.pallas_call(
        put,
        out_shape=(jax.ShapeDtypeStruct(out.shape, BF16), jax.ShapeDtypeStruct(fs.shape, F32)),
        in_specs=[anywhere] * 2,
        out_specs=(anywhere,anywhere),
        scratch_shapes=[dma((5,))],
        compiler_params=pltpu.CompilerParams(vmem_limit_bytes=16 * 1024 * 1024),
    )(out, fs)


def solution(mesh):
    nx = mesh.shape["dp"] // (2 * NZ)
    ny = mesh.shape["tensor"]
    return jax.shard_map(
        functools.partial(body, nx, ny),
        mesh=mesh,
        in_specs=(
            P("dp"),
            P("dp"),
            P("dp", "tensor", None, None),
            P("dp", None, "tensor"),
            P("dp", None, None, "tensor"),
            P("dp", "tensor", None, None),
            P("dp", None, "tensor"),
            P("dp", None, None, "tensor"),
            P(None, "dp", "tensor"),
            P(None, "dp", "tensor"),
            P(None, "dp", None, "tensor"),
            P(None, "dp", "tensor"),
            P(None, "tensor"),
            P(None, None, "tensor"),
            P("tensor"),
            P("tensor"),
            P("tensor"),
            P("tensor"),
        ),
        out_specs=(P(None, "dp", "tensor"), P("dp", "tensor", None, None)),
        check_vma=False,
    )
```

time: 323 us -> 43.9 us (0.14); the launches traced: 316 us -> 43.8 us
  blocking collectives: 283 us -> 0 us
  Pallas kernels: 0 us -> 43.1 us
  between operations: 15.1 us -> 0.65 us
  local copies, waits for them, and re-layouts: 7.25 us -> 0 us
  matrix products: 5.8 us -> 0 us
  other arithmetic: 4.85 us -> 0 us
    psum x2 -> x0, blocking collectives: 259 us -> none  [the longest x1 245 us: body(): lax.psum((part_state, part_x, part_bc), 'dp')]
    pallas_call x0 -> x2, Pallas kernels: none -> 43.1 us  [the longest x1 42.1 us: body(): pl.pallas_call(functools.partial(kernel, nx, ny), out_shape=(pltpu.VMEM((...]
    unnamed x1 -> x0, blocking collectives: 23.9 us -> none
    dot_general x3 -> x0, matrix products: 5.8 us -> none  [body(): jnp.einsum('shpn,shn->shp', state, c_heads, precision=lax.Precision.HIGHEST)]
  transfers between devices with their start and end apart: 1 -> 0, of which waited for: 0 -> 0; matrix products, arithmetic and copies ran while one was open for 1% -> 0% of each run, Pallas kernels for 0% -> 0%
where the time goes in v2:
time: 43.9 us; the launch traced here: 43.8 us
  Pallas kernels  43.1 us (98%)
  between operations  0.65 us (1%)
    pallas_call x1, Pallas kernels, body(): pl.pallas_call(functools.partial(kernel, nx, ny), out_shape=(pltpu.VMEM((...  42.1 us
    pallas_call x1, Pallas kernels, body(): pl.pallas_call(put, out_shape=(jax.ShapeDtypeStruct(out.shape, BF16), jax...  1.01 us

profile of v2, /device:TPU:1, one launch (start us, length us, event | category | flops | bytes accessed | tf_op | source)
XLA Modules:
  0.0 43.8 jit_solution(6270510948408271411)
XLA Ops:
  0.6 42.1 %shard_map.185 = (bf16[3,2,1024]{2,1,0:T(2,128)(2,1)S(1)}, f32[2,16,64,128]{3,2,1,0:T(8,128)S(1)}) custom-call(s32[2]{0:T(128)} %refs_0_.1, s32[2]{0:T(128)} %refs_1_.1, f32[2,16,64,128]{3,2,1,0:T(8,128)} %refs_2_.1, bf16[3,2,1024]{2,1,0:T(2,128)(2,1)} %bitcast.7, bf16[2,3,2,128]{3,2,1,0:T(2,128)(2,1)} %refs_4_.1, bf16[4,16,64,128]{3,2,1,0:T(8,128)(2,1)} %refs_5_.1, ...), custom_call_target="tpu_custom_call" | custom-call | tf_op jit(solution)/shard_map/pallas_call | solution.py:665
  42.8 1.0 %shard_map.186 = (bf16[3,2,1024]{2,1,0:T(2,128)(2,1)}, f32[2,16,64,128]{3,2,1,0:T(8,128)}) custom-call(bf16[3,2,1024]{2,1,0:T(2,128)(2,1)S(1)} %get-tuple-element.4.out_ref, f32[2,16,64,128]{3,2,1,0:T(8,128)S(1)} %get-tuple-element.5.fs_ref), custom_call_target="tpu_custom_call" | custom-call | tf_op jit(solution)/shard_map/pallas_call | solution.py:678

commit v3 on v2

--- a/solution.py
+++ b/solution.py
@@ -144,7 +144,7 @@
         both = dot(c_parts, hi, 1, 1)
         ys.append(both[0:ROWS] + both[ROWS:] + dot(c_parts, lo, 1, 1)[0:ROWS])
     row = lax.broadcasted_iota(jnp.int32, (ROWS, CH), 0)
-    R.base[...] = jnp.where(lax.rem(row, 2) == 0, ys[0], ys[1])
+    R.base[...] = jnp.where(row >= 2 * STEPS, 0.0, jnp.where(lax.rem(row, 2) == 0, ys[0], ys[1]))
 
 
 def sec_unpack(R, packed):
@@ -202,7 +202,6 @@
         R.gub[2 * k : 2 * k + 2] = gs[k]
     for t in range(STEPS):
         R.gate[2 * t : 2 * t + 2] = silu(R.zin[t].astype(F32))
-    R.cparts[...] = stack(split(R.acc[:, CH + STATES :], 3) + [jnp.zeros((ROWS, STATES), F32)], 0)
 
 
 def sec_last(R):
@@ -222,18 +221,69 @@
             )
 
 
-def sec_gate(R):
-    y = dot(R.cparts[...], R.fbuf[...].reshape(CH, STATES), 1, 1)
-    y = y[0:8] + y[8:16] + y[16:24]
-    gated = (R.base[...] + R.bco[...] * y) * R.gate[...]
-    R.base[...] = gated
+def sec_own_c(R, f):
+    rows = [
+        jnp.where(R.fin[0] < STEPS, R.bcin[t, 0, 1:2, :].astype(F32), R.bcin[t, 1, 1:2, :].astype(F32))
+        for t in range(STEPS)
+    ]
+    after = [
+        jnp.where(f == 0, rows[0], jnp.where(f == 1, rows[1], rows[2])),
+        jnp.where(f == 0, rows[1], rows[2]),
+        rows[2],
+    ]
+    for n in range(STEPS):
+        total = jnp.zeros((1, STATES), F32)
+        for i in range(n + 1):
+            total += R.cwbc[i + 3 - n, 1:2, :] * after[i]
+        R.esend[n : n + 1] = total
+        R.esend[n + 4 : n + 5] = total
+
+
+def sec_group_y(R, packed):
+    fork_c = [packed[4 * (2 * i + 1) + 3 : 4 * (2 * i + 1) + 4] for i in range(3)]
+    zero = jnp.zeros((1, STATES), F32)
+    adds = []
+    for n in range(STEPS):
+        total = zero
+        for k in range(3 - n):
+            total += R.cwbc[k, 1:2, :] * fork_c[n + k]
+        adds.append(total)
+    adds = jnp.concatenate((adds + [zero]) * 2, axis=0)
+    cs = silu(R.ebuf[...] + adds[None]).reshape(2 * NZ * 8, STATES)
+    y = dot(stack(split(cs, 2), 0), R.hbuf[...].reshape(HALF * WIDTH, STATES), 1, 1)
+    y = (y[: 2 * NZ * 8] + y[2 * NZ * 8 :]).reshape(2 * NZ, 8, HALF * WIDTH)
+    top = lax.broadcasted_iota(jnp.int32, (2 * NZ, 8, 128), 1) < 4
+    for i in range(2):
+        lo = 256 * i
+        R.yrs[:, 8 * i : 8 * i + 8, :] = jnp.where(
+            top, y[:, :, lo : lo + 128], y[:, :, lo + 128 : lo + 256]
+        )
+
+
+def sec_gate(R, f, owner_z):
+    rows = []
+    for n in range(STEPS):
+        rows.append(
+            jnp.concatenate(
+                [
+                    R.yrb[cc, owner_z, 8 * i + 4 * j + n : 8 * i + 4 * j + n + 1, :]
+                    for cc in range(2)
+                    for i in range(2)
+                    for j in range(2)
+                ],
+                axis=1,
+            )
+        )
+    at_step = [
+        rows[0],
+        jnp.where(f == 0, rows[1], rows[0]),
+        jnp.where(f == 0, rows[2], jnp.where(f == 1, rows[1], rows[0])),
+    ]
+    for t in range(STEPS):
+        two = slice(2 * t, 2 * t + 2)
+        R.base[two] = (R.base[two] + R.bco[two] * at_step[t]) * R.gate[two]
+    gated = R.base[...]
     return jnp.sum(gated * gated, axis=1, keepdims=True)
-
-
-def sec_state(R, h):
-    f = R.fbuf[h].astype(F32)
-    for s in range(2):
-        R.ssm[s, h] = R.ssm[s, h] + R.ab[1, s, h : h + 1, :] * f
 
 
 NAMES = (
@@ -256,7 +306,9 @@
     "skip_hbm",
     "gain_hbm",
     "out",
-    "fs_hbm",
+    "pre_out",
+    "fork_out",
+    "ab_out",
     "ssm",
     "cx",
     "cbc",
@@ -302,7 +354,11 @@
     "gub",
     "gate",
     "ab",
-    "cparts",
+    "esend",
+    "ebuf",
+    "hbuf",
+    "yrs",
+    "yrb",
     "in_sem",
     "sc_sem",
     "own_sem",
@@ -323,6 +379,10 @@
     "g_r",
     "f_s",
     "f_r",
+    "e_s",
+    "e_r",
+    "r_s",
+    "r_r",
     "y_s",
     "y_r",
 )
@@ -363,21 +423,24 @@
         )
 
     barrier = pltpu.get_barrier_semaphore()
-    for d in range(1, ny):
-        pl.semaphore_signal(barrier, inc=1, device_id={"tensor": ypeer(d)}, device_id_type=MESH)
-    for d in range(1, NZ):
-        pl.semaphore_signal(barrier, inc=1, device_id=at(x, zpeer(d), c), device_id_type=MESH)
     for d in range(1, nx):
         pl.semaphore_signal(barrier, inc=1, device_id=at(xpeer(d), z, c), device_id_type=MESH)
-    pl.semaphore_signal(barrier, inc=1, device_id=sibling, device_id_type=MESH)
-
-    mine = pl.ds(pl.multiple_of(c * HALF, HALF), HALF)
-    theirs = pl.ds(pl.multiple_of((1 - c) * HALF, HALF), HALF)
-    my_slot = pl.ds(pl.multiple_of(c * HELD, HELD), HELD)
     scalars = [
         pltpu.make_async_copy(R.fin_hbm, R.fin, R.sc_sem.at[0]),
         pltpu.make_async_copy(R.src_hbm, R.src, R.sc_sem.at[1]),
     ]
+    for cp in scalars:
+        cp.start()
+    for d in (4, 3, 5, 2, 6, 1, 7):
+        for cc in (c, 1 - c):
+            pl.semaphore_signal(barrier, inc=1, device_id=at(x, zpeer(d), cc), device_id_type=MESH)
+    for d in range(1, ny):
+        pl.semaphore_signal(barrier, inc=1, device_id={"tensor": ypeer(d)}, device_id_type=MESH)
+    pl.semaphore_signal(barrier, inc=1, device_id=sibling, device_id_type=MESH)
+
+    mine = pl.ds(pl.multiple_of(c * HALF, HALF), HALF)
+    theirs = pl.ds(pl.multiple_of((1 - c) * HALF, HALF), HALF)
+    my_slot = pl.ds(pl.multiple_of(c * HELD, HELD), HELD)
     loads = [
         pltpu.make_async_copy(src, dst, R.in_sem.at[i])
         for i, (src, dst) in enumerate(
@@ -401,16 +464,13 @@
         )
     ]
     own = pltpu.make_async_copy(R.pssm_hbm.at[:, mine], R.pbuf.at[my_slot], R.own_sem)
-    for cp in scalars + loads[:2] + [own] + loads[2:]:
-        cp.start()
-    for ref in (R.wts, R.st, R.acc, R.base, R.bco, R.gub, R.gate):
-        ref[...] = jnp.zeros_like(ref)
     for cp in scalars:
         cp.wait()
     prompt = jnp.where(R.fin[0] < STEPS, R.src[0], R.src[1])
+    refill = jnp.where(R.fin[0] < STEPS, R.fin[0], R.fin[1])
     R.plan_out[...] = jnp.full(R.plan_out.shape, prompt, jnp.int32)
 
-    pl.semaphore_wait(barrier, 1 + (nx - 1) + (NZ - 1) + (ny - 1))
+    pl.semaphore_wait(barrier, 1 + (nx - 1) + 2 * (NZ - 1) + (ny - 1))
 
     order = (2, 1, 3) if nx == 4 else tuple(range(1, nx))
     plans = {}
@@ -421,6 +481,28 @@
         plans[d].start()
     pair = remote(R.pssm_hbm.at[:, theirs], R.pbuf.at[my_slot], R.pair_s.at[0], R.pair_r.at[0], sibling)
     pair.start()
+    for cp in [loads[9], loads[11], loads[0], loads[1], own] + loads[2:9] + [loads[10]] + loads[12:]:
+        cp.start()
+    for ref in (R.wts, R.st, R.acc, R.base, R.bco, R.gub, R.gate, R.esend):
+        ref[...] = jnp.zeros_like(ref)
+    loads[9].wait()
+    loads[11].wait()
+    sec_own_c(R, refill)
+    here = c * NZ + z
+    R.ebuf[here] = R.esend[...]
+
+    def group(src, dst, ssem, rsem):
+        sends = []
+        for d in (4, 3, 5, 2, 6, 1, 7, 0):
+            for k in (0, 1) if d else (1,):
+                cc = c if k == 0 else 1 - c
+                to = cc * NZ + zpeer(d)
+                cp = remote(src(to), dst, ssem.at[k, d], rsem.at[k, d], at(x, zpeer(d), cc))
+                cp.start()
+                sends.append(cp)
+        return sends
+
+    e_sends = group(lambda to: R.esend, R.ebuf.at[here], R.e_s, R.e_r)
     loads[0].wait()
     loads[1].wait()
     sec_pack(R)
@@ -442,7 +524,7 @@
         plans[d].wait_recv()
 
     def wanted(d):
-        return lax.rem(jnp.max(R.plan_in[nx - d]), 2 * HELD)
+        return lax.rem(R.plan_in[nx - d, 0, 0], 2 * HELD)
 
     want = {d: wanted(d) for d in order}
     want[0] = lax.rem(prompt, 2 * HELD)
@@ -474,7 +556,7 @@
         for n, o in enumerate(offsets):
             xbs[g][x, n] = R.pbuf[want[0], zpeer(o)]
 
-    for i in range(6, 12):
+    for i in (6, 7, 8, 10):
         loads[i].wait()
     sec_seq(R)
 
@@ -497,6 +579,7 @@
             cp.wait_recv()
         for n, o in enumerate(offsets):
             head = xbs[g][owner_x, n]
+            R.hbuf[zpeer(o)] = head
             if o == 0:
                 R.zbuf[z] = head
             else:
@@ -506,6 +589,12 @@
                 )
                 z_sends[o].start()
 
+    for cp in e_sends:
+        cp.wait_recv()
+    sec_group_y(R, picked.astype(F32))
+    r_sends = group(lambda to: R.yrs.at[to], R.yrb.at[c, z], R.r_s, R.r_r)
+    R.yrb[c, z] = R.yrs[here]
+
     for cp in cz_sends:
         cp.wait_recv()
     sec_unpack(R, R.czbuf[owner_z].astype(F32))
@@ -513,7 +602,6 @@
 
     for o in (4, 3, 5, 2, 6, 1, 7):
         z_sends[o].wait_recv()
-    here = c * HALF + z
     R.fbuf[here] = R.zbuf[owner_z]
     g_sends, f_sends = {}, {}
     for d in (4, 3, 5, 2, 6, 1, 7):
@@ -527,6 +615,23 @@
         loads[i].wait()
     sec_mix(R)
     sec_last(R)
+    stores = [
+        pltpu.make_async_copy(R.ssm, R.pre_out, R.out_sem.at[0]),
+        pltpu.make_async_copy(R.ab.at[1], R.ab_out, R.out_sem.at[1]),
+    ]
+    for cp in stores:
+        cp.start()
+
+    for cp in r_sends:
+        cp.wait_recv()
+    R.ysend[...] = jnp.broadcast_to(sec_gate(R, refill, owner_z), R.ysend.shape)
+    R.ybuf[y] = R.ysend[...]
+    y_sends = []
+    for d in (4, 3, 5, 2, 6, 1, 7) if ny == 8 else range(1, ny):
+        cp = remote(R.ysend, R.ybuf.at[y], R.y_s.at[d], R.y_r.at[d], {"tensor": ypeer(d)})
+        cp.start()
+        y_sends.append(cp)
+
     for d in NEAR:
         g_sends[d].wait_recv()
         landed = c * HALF + zpeer(NZ - d)
@@ -535,27 +640,9 @@
     for d in (0,) + NEAR:
         f_sends[d].wait_recv()
 
-    squares = sec_gate(R)
-    R.ysend[...] = jnp.broadcast_to(squares, R.ysend.shape)
-    R.ybuf[y] = R.ysend[...]
-    y_sends = []
-    for d in (4, 3, 5, 2, 6, 1, 7) if ny == 8 else range(1, ny):
-        cp = remote(R.ysend, R.ybuf.at[y], R.y_s.at[d], R.y_r.at[d], {"tensor": ypeer(d)})
-        cp.start()
-        y_sends.append(cp)
-
-    stores = []
-    for h in range(HEADS):
-        sec_state(R, h)
-        if h % 4 == 3:
-            for s in range(2):
-                some = slice(h - 3, h + 1)
-                cp = pltpu.make_async_copy(
-                    R.ssm.at[s, some], R.fs_hbm.at[s, some], R.out_sem.at[s, h // 4]
-                )
-                cp.start()
-                stores.append(cp)
-    for cp in list(plans.values()) + [pair, pair_conv] + conv_sends + cz_sends:
+    fork_copy = pltpu.make_async_copy(R.fbuf, R.fork_out, R.out_sem.at[2])
+    fork_copy.start()
+    for cp in list(plans.values()) + [pair, pair_conv] + conv_sends + cz_sends + e_sends + r_sends:
         cp.wait_send()
     for sends in x_sends:
         for cp in sends:
@@ -563,7 +650,7 @@
     for group in (z_sends, g_sends, f_sends):
         for cp in group.values():
             cp.wait_send()
-    for cp in stores:
+    for cp in stores + [fork_copy]:
         cp.wait()
 
     for cp in y_sends:
@@ -579,15 +666,18 @@
         cp.wait_send()
 
 
-def put(out_ref, fs_ref, out_hbm, fs_hbm, sem):
-    copies = [
-        pltpu.make_async_copy(fs_ref.at[s, h : h + 8], fs_hbm.at[s, h : h + 8], sem.at[2 * s + h // 8])
-        for s in range(2)
-        for h in (0, 8)
-    ]
-    copies.append(pltpu.make_async_copy(out_ref, out_hbm, sem.at[4]))
-    for cp in copies:
+def put(out_ref, pre_ref, fork_ref, ab_ref, out_hbm, fs_hbm, fs, sem):
+    copies = [pltpu.make_async_copy(out_ref, out_hbm, sem.at[0])]
+    copies[0].start()
+    for i in range(4):
+        some = slice(4 * i, 4 * i + 4)
+        for h in range(4 * i, 4 * i + 4):
+            f = fork_ref[h].astype(F32)
+            for s in range(2):
+                fs[s, h] = pre_ref[s, h] + ab_ref[s, h : h + 1, :] * f
+        cp = pltpu.make_async_copy(fs.at[:, some], fs_hbm.at[:, some], sem.at[1 + i])
         cp.start()
+        copies.append(cp)
     for cp in copies:
         cp.wait()
 
@@ -635,11 +725,15 @@
         vmem((ROWS, CH), F32),
         vmem((ROWS, CH), F32),
         vmem((2, 2, HEADS, STATES), F32),
-        vmem((4 * ROWS, STATES), BF16),
+        vmem((8, STATES), F32),
+        vmem((2 * NZ, 8, STATES), F32),
+        vmem((HALF,) + head, BF16),
+        vmem((2 * NZ, 16, 128), F32),
+        vmem((2, NZ, 16, 128), F32),
         dma((len(in_vmem),)),
         dma((2,)),
         dma,
-        dma((2, 4)),
+        dma((3,)),
         dma((nx,)),
         dma((nx,)),
         dma((2,)),
@@ -656,33 +750,40 @@
         dma((NZ,)),
         dma((NZ,)),
         dma((NZ,)),
+        dma((2, NZ)),
+        dma((2, NZ)),
+        dma((2, NZ)),
+        dma((2, NZ)),
         dma((ny,)),
         dma((ny,)),
     ]
     args = [pltpu.with_memory_space_constraint(a, pltpu.HBM) for a in args]
     anywhere = pl.BlockSpec(memory_space=pl.ANY)
     slots = args[0].shape[0]
-    out, fs = pl.pallas_call(
+    out, pre, fork, ab = pl.pallas_call(
         functools.partial(kernel, nx, ny),
         out_shape=(
             pltpu.VMEM((STEPS, slots, CH), BF16),
             pltpu.VMEM(args[2].shape, F32),
+            pltpu.VMEM((HEADS,) + head, BF16),
+            pltpu.VMEM((2, HEADS, STATES), F32),
         ),
         in_specs=[anywhere] * 18,
-        out_specs=(pl.BlockSpec(memory_space=pltpu.VMEM), anywhere),
+        out_specs=(pl.BlockSpec(memory_space=pltpu.VMEM), anywhere, anywhere, anywhere),
         scratch_shapes=scratch,
         compiler_params=pltpu.CompilerParams(
             collective_id=0, has_side_effects=True, vmem_limit_bytes=32 * 1024 * 1024
         ),
     )(*args)
+    inside = pl.BlockSpec(memory_space=pltpu.VMEM)
     return pl.pallas_call(
         put,
-        out_shape=(jax.ShapeDtypeStruct(out.shape, BF16), jax.ShapeDtypeStruct(fs.shape, F32)),
-        in_specs=[anywhere] * 2,
-        out_specs=(anywhere,anywhere),
-        scratch_shapes=[dma((5,))],
+        out_shape=(jax.ShapeDtypeStruct(out.shape, BF16), jax.ShapeDtypeStruct(pre.shape, F32)),
+        in_specs=[anywhere, inside, inside, inside],
+        out_specs=(anywhere, anywhere),
+        scratch_shapes=[vmem(pre.shape, F32), dma((5,))],
         compiler_params=pltpu.CompilerParams(vmem_limit_bytes=16 * 1024 * 1024),
-    )(out, fs)
+    )(out, pre, fork, ab)
 
 
 def solution(mesh):

time: 43.9 us -> 40.3 us (0.918)
  Pallas kernels: 43.1 us -> 39.5 us
    pallas_call x1, Pallas kernels: 42.1 us -> 38.4 us  [body(): pl.pallas_call(functools.partial(kernel, nx, ny), out_shape=(pltpu.VMEM((...]
where the time goes in v3:
time: 40.3 us; the launch traced here: 40.1 us
  Pallas kernels  39.5 us (98%)
  between operations  0.65 us (2%)
    pallas_call x1, Pallas kernels, body(): pl.pallas_call(functools.partial(kernel, nx, ny), out_shape=(pltpu.VMEM((...  38.4 us
    pallas_call x1, Pallas kernels, body(): pl.pallas_call(put, out_shape=(jax.ShapeDtypeStruct(out.shape, BF16), jax...  1.03 us

profile of v3, /device:TPU:1, one launch (start us, length us, event | category | flops | bytes accessed | tf_op | source)
XLA Modules:
  0.0 40.1 jit_solution(10225408666443655590)
XLA Ops:
  0.6 38.4 %shard_map.185 = (bf16[3,2,1024]{2,1,0:T(2,128)(2,1)S(1)}, f32[2,16,64,128]{3,2,1,0:T(8,128)S(1)}, bf16[16,64,128]{2,1,0:T(8,128)(2,1)S(1)}, f32[2,16,128]{2,1,0:T(8,128)S(1)}) custom-call(s32[2]{0:T(128)} %refs_0_.1, s32[2]{0:T(128)} %refs_1_.1, f32[2,16,64,128]{3,2,1,0:T(8,128)} %refs_2_.1, bf16[3,2,1024]{2,1,0:T(2,128)(2,1)} %bitcast.7, ...), custom_call_target="tpu_custom_call" | custom-call | tf_op jit(solution)/shard_map/pallas_call | solution.py:763
  39.1 1.0 %shard_map.186 = (bf16[3,2,1024]{2,1,0:T(2,128)(2,1)}, f32[2,16,64,128]{3,2,1,0:T(8,128)}) custom-call(bf16[3,2,1024]{2,1,0:T(2,128)(2,1)S(1)} %get-tuple-element.6.out_ref, f32[2,16,64,128]{3,2,1,0:T(8,128)S(1)} %get-tuple-element.7.pre_ref, bf16[16,64,128]{2,1,0:T(8,128)(2,1)S(1)} %get-tuple-element.8.fork_ref, f32[2,16,128]{2,1,0:T(8,128)S(1)} %get-tuple-element.9.ab_ref), custom_call_target="tpu_custom_call" | custom-call | tf_op jit(solution)/shard_map/pallas_call | solution.py:779

commit v4 on v3

--- a/solution.py
+++ b/solution.py
@@ -379,6 +379,8 @@
     "g_r",
     "f_s",
     "f_r",
+    "zrel",
+    "yrel",
     "e_s",
     "e_r",
     "r_s",
@@ -431,12 +433,23 @@
     ]
     for cp in scalars:
         cp.start()
-    for d in (4, 3, 5, 2, 6, 1, 7):
-        for cc in (c, 1 - c):
-            pl.semaphore_signal(barrier, inc=1, device_id=at(x, zpeer(d), cc), device_id_type=MESH)
-    for d in range(1, ny):
-        pl.semaphore_signal(barrier, inc=1, device_id={"tensor": ypeer(d)}, device_id_type=MESH)
+    around = [(R.zrel, at(x, zpeer(1), c), at(x, zpeer(NZ - 1), c))]
+    if ny > 1:
+        around.append((R.yrel, {"tensor": ypeer(1)}, {"tensor": ypeer(ny - 1)}))
+    for _, up, down in around:
+        pl.semaphore_signal(barrier, inc=1, device_id=up, device_id_type=MESH)
+        pl.semaphore_signal(barrier, inc=1, device_id=down, device_id_type=MESH)
     pl.semaphore_signal(barrier, inc=1, device_id=sibling, device_id_type=MESH)
+
+    def tell(n):
+        for sem, up, down in around:
+            pl.semaphore_signal(sem.at[n, 0], inc=1, device_id=up, device_id_type=MESH)
+            pl.semaphore_signal(sem.at[n, 1], inc=1, device_id=down, device_id_type=MESH)
+
+    def hear(n):
+        for sem, _, _ in around:
+            pl.semaphore_wait(sem.at[n, 0], 1)
+            pl.semaphore_wait(sem.at[n, 1], 1)
 
     mine = pl.ds(pl.multiple_of(c * HALF, HALF), HALF)
     theirs = pl.ds(pl.multiple_of((1 - c) * HALF, HALF), HALF)
@@ -470,7 +483,7 @@
     refill = jnp.where(R.fin[0] < STEPS, R.fin[0], R.fin[1])
     R.plan_out[...] = jnp.full(R.plan_out.shape, prompt, jnp.int32)
 
-    pl.semaphore_wait(barrier, 1 + (nx - 1) + 2 * (NZ - 1) + (ny - 1))
+    pl.semaphore_wait(barrier, 1 + (nx - 1) + 2 * len(around))
 
     order = (2, 1, 3) if nx == 4 else tuple(range(1, nx))
     plans = {}
@@ -479,6 +492,7 @@
             R.plan_out, R.plan_in.at[d], R.plan_s.at[d], R.plan_r.at[d], at(xpeer(d), z, c)
         )
         plans[d].start()
+    tell(0)
     pair = remote(R.pssm_hbm.at[:, theirs], R.pbuf.at[my_slot], R.pair_s.at[0], R.pair_r.at[0], sibling)
     pair.start()
     for cp in [loads[9], loads[11], loads[0], loads[1], own] + loads[2:9] + [loads[10]] + loads[12:]:
@@ -502,7 +516,6 @@
                 sends.append(cp)
         return sends
 
-    e_sends = group(lambda to: R.esend, R.ebuf.at[here], R.e_s, R.e_r)
     loads[0].wait()
     loads[1].wait()
     sec_pack(R)
@@ -517,6 +530,8 @@
     sec_dt(R)
     sec_ab(R)
 
+    hear(0)
+    tell(1)
     pair.wait_recv()
     pair_conv.wait_recv()
     own.wait()
@@ -560,6 +575,15 @@
         loads[i].wait()
     sec_seq(R)
 
+    hear(1)
+    tell(2)
+    hear(2)
+    e_sends = []
+    for d in (4, 3, 5, 2, 6, 1, 7):
+        cp = remote(R.esend, R.ebuf.at[here], R.e_s.at[d], R.e_r.at[d], at(x, zpeer(d), c))
+        cp.start()
+        e_sends.append(cp)
+
     for cp in conv_sends:
         cp.wait_recv()
     picked = R.cxbuf[owner_x]
@@ -572,6 +596,11 @@
         cz_sends.append(cp)
     loads[14].wait()
     sec_old(R)
+
+    for cp in e_sends:
+        cp.wait_recv()
+    swap_c = remote(R.ebuf.at[mine], R.ebuf.at[mine], R.e_s.at[0], R.e_r.at[0], sibling)
+    swap_c.start()
 
     z_sends = {}
     for g, offsets in enumerate(STAGES):
@@ -589,8 +618,7 @@
                 )
                 z_sends[o].start()
 
-    for cp in e_sends:
-        cp.wait_recv()
+    swap_c.wait_recv()
     sec_group_y(R, picked.astype(F32))
     r_sends = group(lambda to: R.yrs.at[to], R.yrb.at[c, z], R.r_s, R.r_r)
     R.yrb[c, z] = R.yrs[here]
@@ -603,14 +631,12 @@
     for o in (4, 3, 5, 2, 6, 1, 7):
         z_sends[o].wait_recv()
     R.fbuf[here] = R.zbuf[owner_z]
-    g_sends, f_sends = {}, {}
+    g_sends = {}
     for d in (4, 3, 5, 2, 6, 1, 7):
         g_sends[d] = remote(
             R.fbuf.at[here], R.fbuf.at[here], R.g_s.at[d], R.g_r.at[d], at(x, zpeer(d), c)
         )
         g_sends[d].start()
-    f_sends[0] = remote(R.fbuf.at[here], R.fbuf.at[here], R.f_s.at[0], R.f_r.at[0], sibling)
-    f_sends[0].start()
     for i in (12, 13):
         loads[i].wait()
     sec_mix(R)
@@ -634,23 +660,23 @@
 
     for d in NEAR:
         g_sends[d].wait_recv()
-        landed = c * HALF + zpeer(NZ - d)
-        f_sends[d] = remote(R.fbuf.at[landed], R.fbuf.at[landed], R.f_s.at[d], R.f_r.at[d], sibling)
-        f_sends[d].start()
-    for d in (0,) + NEAR:
-        f_sends[d].wait_recv()
-
-    fork_copy = pltpu.make_async_copy(R.fbuf, R.fork_out, R.out_sem.at[2])
-    fork_copy.start()
-    for cp in list(plans.values()) + [pair, pair_conv] + conv_sends + cz_sends + e_sends + r_sends:
+    swap = remote(R.fbuf.at[mine], R.fbuf.at[mine], R.f_s, R.f_r, sibling)
+    swap.start()
+    stores.append(pltpu.make_async_copy(R.fbuf.at[mine], R.fork_out.at[mine], R.out_sem.at[2]))
+    stores[-1].start()
+    swap.wait_recv()
+    stores.append(pltpu.make_async_copy(R.fbuf.at[theirs], R.fork_out.at[theirs], R.out_sem.at[3]))
+    stores[-1].start()
+    for cp in list(plans.values()) + [pair, pair_conv] + conv_sends + cz_sends + e_sends + r_sends + [swap_c]:
         cp.wait_send()
     for sends in x_sends:
         for cp in sends:
             cp.wait_send()
-    for group in (z_sends, g_sends, f_sends):
-        for cp in group.values():
+    for sends in (z_sends, g_sends):
+        for cp in sends.values():
             cp.wait_send()
-    for cp in stores + [fork_copy]:
+    swap.wait_send()
+    for cp in stores:
         cp.wait()
 
     for cp in y_sends:
@@ -733,7 +759,7 @@
         dma((len(in_vmem),)),
         dma((2,)),
         dma,
-        dma((3,)),
+        dma((4,)),
         dma((nx,)),
         dma((nx,)),
         dma((2,)),
@@ -748,10 +774,12 @@
         dma((NZ,)),
         dma((NZ,)),
         dma((NZ,)),
+        dma,
+        dma,
+        pltpu.SemaphoreType.REGULAR((3, 2)),
+        pltpu.SemaphoreType.REGULAR((3, 2)),
         dma((NZ,)),
         dma((NZ,)),
-        dma((2, NZ)),
-        dma((2, NZ)),
         dma((2, NZ)),
         dma((2, NZ)),
         dma((ny,)),

time: 40.3 us -> 39.5 us (0.980)
  Pallas kernels: 39.5 us -> 38.7 us
    pallas_call x1, Pallas kernels: 38.4 us -> 37.7 us  [body(): pl.pallas_call(functools.partial(kernel, nx, ny), out_shape=(pltpu.VMEM((...]
where the time goes in v4:
time: 39.5 us; the launch traced here: 39.4 us
  Pallas kernels  38.7 us (98%)
  between operations  0.65 us (2%)
    pallas_call x1, Pallas kernels, body(): pl.pallas_call(functools.partial(kernel, nx, ny), out_shape=(pltpu.VMEM((...  37.7 us
    pallas_call x1, Pallas kernels, body(): pl.pallas_call(put, out_shape=(jax.ShapeDtypeStruct(out.shape, BF16), jax...  1.03 us

profile of v4, /device:TPU:1, one launch (start us, length us, event | category | flops | bytes accessed | tf_op | source)
XLA Modules:
  0.0 39.4 jit_solution(5382147320758622165)
XLA Ops:
  0.6 37.7 %shard_map.185 = (bf16[3,2,1024]{2,1,0:T(2,128)(2,1)S(1)}, f32[2,16,64,128]{3,2,1,0:T(8,128)S(1)}, bf16[16,64,128]{2,1,0:T(8,128)(2,1)S(1)}, f32[2,16,128]{2,1,0:T(8,128)S(1)}) custom-call(s32[2]{0:T(128)} %refs_0_.1, s32[2]{0:T(128)} %refs_1_.1, f32[2,16,64,128]{3,2,1,0:T(8,128)} %refs_2_.1, bf16[3,2,1024]{2,1,0:T(2,128)(2,1)} %bitcast.7, ...), custom_call_target="tpu_custom_call" | custom-call | tf_op jit(solution)/shard_map/pallas_call | solution.py:791
  38.3 1.0 %shard_map.186 = (bf16[3,2,1024]{2,1,0:T(2,128)(2,1)}, f32[2,16,64,128]{3,2,1,0:T(8,128)}) custom-call(bf16[3,2,1024]{2,1,0:T(2,128)(2,1)S(1)} %get-tuple-element.6.out_ref, f32[2,16,64,128]{3,2,1,0:T(8,128)S(1)} %get-tuple-element.7.pre_ref, bf16[16,64,128]{2,1,0:T(8,128)(2,1)S(1)} %get-tuple-element.8.fork_ref, f32[2,16,128]{2,1,0:T(8,128)S(1)} %get-tuple-element.9.ab_ref), custom_call_target="tpu_custom_call" | custom-call | tf_op jit(solution)/shard_map/pallas_call | solution.py:807

commit v5 on v4

--- a/solution.py
+++ b/solution.py
@@ -433,23 +433,29 @@
     ]
     for cp in scalars:
         cp.start()
-    around = [(R.zrel, at(x, zpeer(1), c), at(x, zpeer(NZ - 1), c))]
-    if ny > 1:
-        around.append((R.yrel, {"tensor": ypeer(1)}, {"tensor": ypeer(ny - 1)}))
-    for _, up, down in around:
-        pl.semaphore_signal(barrier, inc=1, device_id=up, device_id_type=MESH)
-        pl.semaphore_signal(barrier, inc=1, device_id=down, device_id_type=MESH)
+    for d in (1, 2, NZ - 2, NZ - 1):
+        pl.semaphore_signal(barrier, inc=1, device_id=at(x, zpeer(d), c), device_id_type=MESH)
+    for d in (1, ny - 1) if ny > 1 else ():
+        pl.semaphore_signal(barrier, inc=1, device_id={"tensor": ypeer(d)}, device_id_type=MESH)
     pl.semaphore_signal(barrier, inc=1, device_id=sibling, device_id_type=MESH)
 
-    def tell(n):
-        for sem, up, down in around:
-            pl.semaphore_signal(sem.at[n, 0], inc=1, device_id=up, device_id_type=MESH)
-            pl.semaphore_signal(sem.at[n, 1], inc=1, device_id=down, device_id_type=MESH)
-
-    def hear(n):
-        for sem, _, _ in around:
-            pl.semaphore_wait(sem.at[n, 0], 1)
-            pl.semaphore_wait(sem.at[n, 1], 1)
+    def tell_z():
+        for i, d in enumerate((2, NZ - 2)):
+            pl.semaphore_signal(R.zrel.at[i], inc=1, device_id=at(x, zpeer(d), c), device_id_type=MESH)
+
+    def hear_z():
+        for i in range(2):
+            pl.semaphore_wait(R.zrel.at[i], 1)
+
+    def tell_y(n):
+        for i, d in enumerate((1, ny - 1) if ny > 1 else ()):
+            pl.semaphore_signal(
+                R.yrel.at[n, i], inc=1, device_id={"tensor": ypeer(d)}, device_id_type=MESH
+            )
+
+    def hear_y(n):
+        for i in range(2 if ny > 1 else 0):
+            pl.semaphore_wait(R.yrel.at[n, i], 1)
 
     mine = pl.ds(pl.multiple_of(c * HALF, HALF), HALF)
     theirs = pl.ds(pl.multiple_of((1 - c) * HALF, HALF), HALF)
@@ -483,7 +489,7 @@
     refill = jnp.where(R.fin[0] < STEPS, R.fin[0], R.fin[1])
     R.plan_out[...] = jnp.full(R.plan_out.shape, prompt, jnp.int32)
 
-    pl.semaphore_wait(barrier, 1 + (nx - 1) + 2 * len(around))
+    pl.semaphore_wait(barrier, 1 + (nx - 1) + 4 + (2 if ny > 1 else 0))
 
     order = (2, 1, 3) if nx == 4 else tuple(range(1, nx))
     plans = {}
@@ -492,7 +498,8 @@
             R.plan_out, R.plan_in.at[d], R.plan_s.at[d], R.plan_r.at[d], at(xpeer(d), z, c)
         )
         plans[d].start()
-    tell(0)
+    tell_z()
+    tell_y(0)
     pair = remote(R.pssm_hbm.at[:, theirs], R.pbuf.at[my_slot], R.pair_s.at[0], R.pair_r.at[0], sibling)
     pair.start()
     for cp in [loads[9], loads[11], loads[0], loads[1], own] + loads[2:9] + [loads[10]] + loads[12:]:
@@ -525,13 +532,15 @@
     )
     pair_conv.start()
 
-    for i in range(2, 6):
-        loads[i].wait()
-    sec_dt(R)
-    sec_ab(R)
-
-    hear(0)
-    tell(1)
+    hear_z()
+    e_sends = []
+    for d in (4, 3, 5, 2, 6, 1, 7):
+        cp = remote(R.esend, R.ebuf.at[here], R.e_s.at[d], R.e_r.at[d], at(x, zpeer(d), c))
+        cp.start()
+        e_sends.append(cp)
+
+    hear_y(0)
+    tell_y(1)
     pair.wait_recv()
     pair_conv.wait_recv()
     own.wait()
@@ -574,16 +583,13 @@
     for i in (6, 7, 8, 10):
         loads[i].wait()
     sec_seq(R)
-
-    hear(1)
-    tell(2)
-    hear(2)
-    e_sends = []
-    for d in (4, 3, 5, 2, 6, 1, 7):
-        cp = remote(R.esend, R.ebuf.at[here], R.e_s.at[d], R.e_r.at[d], at(x, zpeer(d), c))
-        cp.start()
-        e_sends.append(cp)
-
+    for i in range(2, 6):
+        loads[i].wait()
+    sec_dt(R)
+    sec_ab(R)
+
+    hear_y(1)
+    tell_y(2)
     for cp in conv_sends:
         cp.wait_recv()
     picked = R.cxbuf[owner_x]
@@ -594,13 +600,11 @@
         cp = remote(R.czsend, R.czbuf.at[z], R.cz_s.at[d], R.cz_r.at[d], at(x, zpeer(d), c))
         cp.start()
         cz_sends.append(cp)
-    loads[14].wait()
-    sec_old(R)
-
     for cp in e_sends:
         cp.wait_recv()
     swap_c = remote(R.ebuf.at[mine], R.ebuf.at[mine], R.e_s.at[0], R.e_r.at[0], sibling)
     swap_c.start()
+
 
     z_sends = {}
     for g, offsets in enumerate(STAGES):
@@ -622,6 +626,8 @@
     sec_group_y(R, picked.astype(F32))
     r_sends = group(lambda to: R.yrs.at[to], R.yrb.at[c, z], R.r_s, R.r_r)
     R.yrb[c, z] = R.yrs[here]
+    loads[14].wait()
+    sec_old(R)
 
     for cp in cz_sends:
         cp.wait_recv()
@@ -632,7 +638,7 @@
         z_sends[o].wait_recv()
     R.fbuf[here] = R.zbuf[owner_z]
     g_sends = {}
-    for d in (4, 3, 5, 2, 6, 1, 7):
+    for d in (1, 7, 2, 6, 3, 5, 4):
         g_sends[d] = remote(
             R.fbuf.at[here], R.fbuf.at[here], R.g_s.at[d], R.g_r.at[d], at(x, zpeer(d), c)
         )
@@ -651,6 +657,7 @@
     for cp in r_sends:
         cp.wait_recv()
     R.ysend[...] = jnp.broadcast_to(sec_gate(R, refill, owner_z), R.ysend.shape)
+    hear_y(2)
     R.ybuf[y] = R.ysend[...]
     y_sends = []
     for d in (4, 3, 5, 2, 6, 1, 7) if ny == 8 else range(1, ny):
@@ -776,7 +783,7 @@
         dma((NZ,)),
         dma,
         dma,
-        pltpu.SemaphoreType.REGULAR((3, 2)),
+        pltpu.SemaphoreType.REGULAR((2,)),
         pltpu.SemaphoreType.REGULAR((3, 2)),
         dma((NZ,)),
         dma((NZ,)),

time: 39.5 us -> 39.2 us (level)
  no operation moved by 1% of the time
where the time goes in v5:
time: 39.2 us; the launch traced here: 39.1 us
  Pallas kernels  38.4 us (98%)
  between operations  0.65 us (2%)
    pallas_call x1, Pallas kernels, body(): pl.pallas_call(functools.partial(kernel, nx, ny), out_shape=(pltpu.VMEM((...  37.4 us
    pallas_call x1, Pallas kernels, body(): pl.pallas_call(put, out_shape=(jax.ShapeDtypeStruct(out.shape, BF16), jax...  1.03 us

profile of v5, /device:TPU:1, one launch (start us, length us, event | category | flops | bytes accessed | tf_op | source)
XLA Modules:
  0.0 39.1 jit_solution(2874989473855159971)
XLA Ops:
  0.6 37.4 %shard_map.185 = (bf16[3,2,1024]{2,1,0:T(2,128)(2,1)S(1)}, f32[2,16,64,128]{3,2,1,0:T(8,128)S(1)}, bf16[16,64,128]{2,1,0:T(8,128)(2,1)S(1)}, f32[2,16,128]{2,1,0:T(8,128)S(1)}) custom-call(s32[2]{0:T(128)} %refs_0_.1, s32[2]{0:T(128)} %refs_1_.1, f32[2,16,64,128]{3,2,1,0:T(8,128)} %refs_2_.1, bf16[3,2,1024]{2,1,0:T(2,128)(2,1)} %bitcast.7, ...), custom_call_target="tpu_custom_call" | custom-call | tf_op jit(solution)/shard_map/pallas_call | solution.py:798
  38.0 1.0 %shard_map.186 = (bf16[3,2,1024]{2,1,0:T(2,128)(2,1)}, f32[2,16,64,128]{3,2,1,0:T(8,128)}) custom-call(bf16[3,2,1024]{2,1,0:T(2,128)(2,1)S(1)} %get-tuple-element.6.out_ref, f32[2,16,64,128]{3,2,1,0:T(8,128)S(1)} %get-tuple-element.7.pre_ref, bf16[16,64,128]{2,1,0:T(8,128)(2,1)S(1)} %get-tuple-element.8.fork_ref, f32[2,16,128]{2,1,0:T(8,128)S(1)} %get-tuple-element.9.ab_ref), custom_call_target="tpu_custom_call" | custom-call | tf_op jit(solution)/shard_map/pallas_call | solution.py:814

commit v6 on v5

--- a/solution.py
+++ b/solution.py
@@ -236,7 +236,6 @@
         for i in range(n + 1):
             total += R.cwbc[i + 3 - n, 1:2, :] * after[i]
         R.esend[n : n + 1] = total
-        R.esend[n + 4 : n + 5] = total
 
 
 def sec_group_y(R, packed):
@@ -248,16 +247,13 @@
         for k in range(3 - n):
             total += R.cwbc[k, 1:2, :] * fork_c[n + k]
         adds.append(total)
-    adds = jnp.concatenate((adds + [zero]) * 2, axis=0)
+    adds = jnp.concatenate(adds + [zero] * 5, axis=0)
     cs = silu(R.ebuf[...] + adds[None]).reshape(2 * NZ * 8, STATES)
     y = dot(stack(split(cs, 2), 0), R.hbuf[...].reshape(HALF * WIDTH, STATES), 1, 1)
     y = (y[: 2 * NZ * 8] + y[2 * NZ * 8 :]).reshape(2 * NZ, 8, HALF * WIDTH)
-    top = lax.broadcasted_iota(jnp.int32, (2 * NZ, 8, 128), 1) < 4
-    for i in range(2):
-        lo = 256 * i
-        R.yrs[:, 8 * i : 8 * i + 8, :] = jnp.where(
-            top, y[:, :, lo : lo + 128], y[:, :, lo + 128 : lo + 256]
-        )
+    for n in range(STEPS):
+        for q in range(4):
+            R.yrs[:, n, q, :] = y[:, n, 128 * q : 128 * (q + 1)]
 
 
 def sec_gate(R, f, owner_z):
@@ -266,10 +262,9 @@
         rows.append(
             jnp.concatenate(
                 [
-                    R.yrb[cc, owner_z, 8 * i + 4 * j + n : 8 * i + 4 * j + n + 1, :]
+                    R.yrb[cc, owner_z, n, q : q + 1, :]
                     for cc in range(2)
-                    for i in range(2)
-                    for j in range(2)
+                    for q in range(4)
                 ],
                 axis=1,
             )
@@ -761,8 +756,8 @@
         vmem((8, STATES), F32),
         vmem((2 * NZ, 8, STATES), F32),
         vmem((HALF,) + head, BF16),
-        vmem((2 * NZ, 16, 128), F32),
-        vmem((2, NZ, 16, 128), F32),
+        vmem((2 * NZ, STEPS, 4, 128), F32),
+        vmem((2, NZ, STEPS, 4, 128), F32),
         dma((len(in_vmem),)),
         dma((2,)),
         dma,

time: 39.2 us -> 38.3 us (0.977)
  Pallas kernels: 38.4 us -> 37.5 us
    pallas_call x1, Pallas kernels: 37.4 us -> 36.4 us  [body(): pl.pallas_call(functools.partial(kernel, nx, ny), out_shape=(pltpu.VMEM((...]
where the time goes in v6:
time: 38.3 us; the launch traced here: 38.1 us
  Pallas kernels  37.5 us (98%)
  between operations  0.65 us (2%)
    pallas_call x1, Pallas kernels, body(): pl.pallas_call(functools.partial(kernel, nx, ny), out_shape=(pltpu.VMEM((...  36.4 us
    pallas_call x1, Pallas kernels, body(): pl.pallas_call(put, out_shape=(jax.ShapeDtypeStruct(out.shape, BF16), jax...  1.03 us

profile of v6, /device:TPU:1, one launch (start us, length us, event | category | flops | bytes accessed | tf_op | source)
XLA Modules:
  0.0 38.1 jit_solution(16224617099832166606)
XLA Ops:
  0.6 36.4 %shard_map.185 = (bf16[3,2,1024]{2,1,0:T(2,128)(2,1)S(1)}, f32[2,16,64,128]{3,2,1,0:T(8,128)S(1)}, bf16[16,64,128]{2,1,0:T(8,128)(2,1)S(1)}, f32[2,16,128]{2,1,0:T(8,128)S(1)}) custom-call(s32[2]{0:T(128)} %refs_0_.1, s32[2]{0:T(128)} %refs_1_.1, f32[2,16,64,128]{3,2,1,0:T(8,128)} %refs_2_.1, bf16[3,2,1024]{2,1,0:T(2,128)(2,1)} %bitcast.7, ...), custom_call_target="tpu_custom_call" | custom-call | tf_op jit(solution)/shard_map/pallas_call | solution.py:793
  37.1 1.0 %shard_map.186 = (bf16[3,2,1024]{2,1,0:T(2,128)(2,1)}, f32[2,16,64,128]{3,2,1,0:T(8,128)}) custom-call(bf16[3,2,1024]{2,1,0:T(2,128)(2,1)S(1)} %get-tuple-element.6.out_ref, f32[2,16,64,128]{3,2,1,0:T(8,128)S(1)} %get-tuple-element.7.pre_ref, bf16[16,64,128]{2,1,0:T(8,128)(2,1)S(1)} %get-tuple-element.8.fork_ref, f32[2,16,128]{2,1,0:T(8,128)S(1)} %get-tuple-element.9.ab_ref), custom_call_target="tpu_custom_call" | custom-call | tf_op jit(solution)/shard_map/pallas_call | solution.py:809

commit v7 on v6

--- a/solution.py
+++ b/solution.py
@@ -248,7 +248,8 @@
             total += R.cwbc[k, 1:2, :] * fork_c[n + k]
         adds.append(total)
     adds = jnp.concatenate(adds + [zero] * 5, axis=0)
-    cs = silu(R.ebuf[...] + adds[None]).reshape(2 * NZ * 8, STATES)
+    R.epad[:, 0:4, :] = R.ebuf[...]
+    cs = silu(R.epad[...] + adds[None]).reshape(2 * NZ * 8, STATES)
     y = dot(stack(split(cs, 2), 0), R.hbuf[...].reshape(HALF * WIDTH, STATES), 1, 1)
     y = (y[: 2 * NZ * 8] + y[2 * NZ * 8 :]).reshape(2 * NZ, 8, HALF * WIDTH)
     for n in range(STEPS):
@@ -351,6 +352,7 @@
     "ab",
     "esend",
     "ebuf",
+    "epad",
     "hbuf",
     "yrs",
     "yrb",
@@ -499,7 +501,7 @@
     pair.start()
     for cp in [loads[9], loads[11], loads[0], loads[1], own] + loads[2:9] + [loads[10]] + loads[12:]:
         cp.start()
-    for ref in (R.wts, R.st, R.acc, R.base, R.bco, R.gub, R.gate, R.esend):
+    for ref in (R.wts, R.st, R.acc, R.base, R.bco, R.gub, R.gate, R.esend, R.epad):
         ref[...] = jnp.zeros_like(ref)
     loads[9].wait()
     loads[11].wait()
@@ -753,7 +755,8 @@
         vmem((ROWS, CH), F32),
         vmem((ROWS, CH), F32),
         vmem((2, 2, HEADS, STATES), F32),
-        vmem((8, STATES), F32),
+        vmem((4, STATES), F32),
+        vmem((2 * NZ, 4, STATES), F32),
         vmem((2 * NZ, 8, STATES), F32),
         vmem((HALF,) + head, BF16),
         vmem((2 * NZ, STEPS, 4, 128), F32),

time: 38.3 us -> 38.3 us (level)
  no operation moved by 1% of the time
where the time goes in v7:
time: 38.3 us; the launch traced here: 38.1 us
  Pallas kernels  37.5 us (98%)
  between operations  0.65 us (2%)
    pallas_call x1, Pallas kernels, body(): pl.pallas_call(functools.partial(kernel, nx, ny), out_shape=(pltpu.VMEM((...  36.4 us
    pallas_call x1, Pallas kernels, body(): pl.pallas_call(put, out_shape=(jax.ShapeDtypeStruct(out.shape, BF16), jax...  1.03 us

profile of v7, /device:TPU:1, one launch (start us, length us, event | category | flops | bytes accessed | tf_op | source)
XLA Modules:
  0.0 38.1 jit_solution(8094874297129874966)
XLA Ops:
  0.6 36.4 %shard_map.185 = (bf16[3,2,1024]{2,1,0:T(2,128)(2,1)S(1)}, f32[2,16,64,128]{3,2,1,0:T(8,128)S(1)}, bf16[16,64,128]{2,1,0:T(8,128)(2,1)S(1)}, f32[2,16,128]{2,1,0:T(8,128)S(1)}) custom-call(s32[2]{0:T(128)} %refs_0_.1, s32[2]{0:T(128)} %refs_1_.1, f32[2,16,64,128]{3,2,1,0:T(8,128)} %refs_2_.1, bf16[3,2,1024]{2,1,0:T(2,128)(2,1)} %bitcast.7, ...), custom_call_target="tpu_custom_call" | custom-call | tf_op jit(solution)/shard_map/pallas_call | solution.py:796
  37.1 1.0 %shard_map.186 = (bf16[3,2,1024]{2,1,0:T(2,128)(2,1)}, f32[2,16,64,128]{3,2,1,0:T(8,128)}) custom-call(bf16[3,2,1024]{2,1,0:T(2,128)(2,1)S(1)} %get-tuple-element.6.out_ref, f32[2,16,64,128]{3,2,1,0:T(8,128)S(1)} %get-tuple-element.7.pre_ref, bf16[16,64,128]{2,1,0:T(8,128)(2,1)S(1)} %get-tuple-element.8.fork_ref, f32[2,16,128]{2,1,0:T(8,128)S(1)} %get-tuple-element.9.ab_ref), custom_call_target="tpu_custom_call" | custom-call | tf_op jit(solution)/shard_map/pallas_call | solution.py:812
